TPU v7x, 512 devices: a whole 4x8x8 slice. The times are simulated.
512 devices in a mesh: col: 128 (over z, y, core), lev: 4 (over x).
Axes of the slice: x: 4, y: 8, z: 8, core: 2. Of those that a mesh axis runs over, the one named last changes fastest.
Arguments:
- state: bfloat16 [10, 128, 65536], P(None, 'lev', 'col'), may hold values from -6 to 6
- level_coupling: bfloat16 [10, 128, 128], replicated, may hold values from -0.5 to 0.5
- gwd_in: bfloat16 [1280, 512], replicated, may hold values from -0.15625 to 0.15625
- gwd_out: bfloat16 [512, 256], replicated, may hold values from -0.25 to 0.25
- sw_in: bfloat16 [1280, 512], replicated, may hold values from -0.15625 to 0.15625
- sw_out: bfloat16 [512, 128], replicated, may hold values from -0.25 to 0.25
- phys_device: int32 [16384], P('col'), may hold values from 0 to 127, as said below
- sunlit: int32 [16384], P('col'), may hold values from 0 to 1, as said below
Outputs:
- tendency: bfloat16 [10, 128, 65536], P(None, 'lev', 'col')
- sunlit_heating: bfloat16 [128, 32768], P(None, ('col', 'lev'))
Inputs may be any that keep to these rules, and one draw needn't show every extreme that they name: The sunlit blocks form one cyclic run of half of the 16384 blocks in global order. `phys_device`: the 128 blocks of one dynamics device (blocks d * 128 to d * 128 + 127) go to 128 different physics devices, and every physics device receives exactly 64 sunlit blocks.
All inputs are finite; a program needn't handle non-finite values.
Results may differ from a plain program's by a relative error of at most 0.0045.
Values may be sent and summed in bfloat16 or wider, within the bound.
No kernel may reach another device: no remote copies, remote signals or barrier semaphores. Data moves between devices by JAX's collectives and lax.ppermute only.
A program may use at most 64 MiB of HBM per device.

v0:
```python
import jax
import jax.numpy as jnp
from jax import lax
from jax.sharding import PartitionSpec as P


def shortwave(sw_in, sw_out, columns_data):
    contract = (((0,), (0,)), ((), ()))
    sw_hidden = jnp.tanh(
        lax.dot_general(sw_in, columns_data, contract, preferred_element_type=jnp.float32)
    ).astype(jnp.bfloat16)
    return lax.dot_general(sw_out, sw_hidden, contract, preferred_element_type=jnp.float32)


def column_terms(level_coupling, gwd_in, gwd_out, physical):
    fields, levels, columns = physical.shape
    stacked = physical.reshape(fields * levels, columns)
    coupled = jnp.einsum(
        "fij,fjn->fin", level_coupling, physical, preferred_element_type=jnp.float32
    )
    contract = (((0,), (0,)), ((), ()))
    drag_hidden = jnp.tanh(
        lax.dot_general(gwd_in, stacked, contract, preferred_element_type=jnp.float32)
    ).astype(jnp.bfloat16)
    drag_rows = lax.dot_general(
        gwd_out, drag_hidden, contract, preferred_element_type=jnp.float32
    ).reshape(2, levels, columns)
    return (stacked, coupled, drag_rows)


def combine_terms(coupled, drag_rows, heating):
    fields, levels, columns = coupled.shape
    additions = jnp.concatenate(
        [drag_rows, heating[None], jnp.zeros((fields - 3, levels, columns), jnp.float32)], axis=0
    )
    return (coupled + additions).astype(jnp.bfloat16)


def local(state, level_coupling, gwd_in, gwd_out, sw_in, sw_out, phys_device, sunlit):
    fields, local_levels, local_cols = state.shape
    blocks = phys_device.shape[0]
    block_cols = local_cols // blocks
    lev_count = lax.axis_size("lev")
    levels = local_levels * lev_count
    quarter = block_cols // lev_count
    columns = blocks * quarter
    slot_ids = jnp.arange(blocks, dtype=jnp.int32)
    onehot = (phys_device[None, :] == slot_ids[:, None]).astype(jnp.int32)
    sorting = jnp.sum(onehot * slot_ids[None, :], axis=1)
    flag_sorted = jnp.take(sunlit, sorting)
    grouped = jnp.take(state.reshape(fields, local_levels, blocks, block_cols), sorting, axis=2)
    flag_tiles = jnp.broadcast_to(flag_sorted[None, None, :, None], (1, 1, blocks, lev_count))
    arrived, flag_arrived = (
        lax.all_to_all(
            lax.all_to_all(grouped, "col", split_axis=2, concat_axis=2, tiled=True),
            "lev",
            split_axis=3,
            concat_axis=1,
            tiled=True,
        ),
        lax.all_to_all(
            lax.all_to_all(flag_tiles, "col", split_axis=2, concat_axis=2, tiled=True),
            "lev",
            split_axis=3,
            concat_axis=1,
            tiled=True,
        ),
    )
    lit_flags = flag_arrived[0, 0, :, 0]
    physical = arrived.reshape(fields, levels, columns)
    stacked, coupled, drag_rows = column_terms(level_coupling, gwd_in, gwd_out, physical)
    picked = jnp.argsort(1 - lit_flags, stable=True)[: blocks // 2]
    all_heat = shortwave(sw_in, sw_out, stacked)
    lit_mask = jnp.repeat(lit_flags.astype(jnp.float32), quarter)
    heating = all_heat * lit_mask[None, :]
    heat_blocks = jnp.take(all_heat.reshape(levels, blocks, quarter), picked, axis=1)
    tendency = combine_terms(coupled, drag_rows, heating)
    returned = lax.all_to_all(
        lax.all_to_all(
            tendency.reshape(fields, levels, blocks, quarter),
            "lev",
            split_axis=1,
            concat_axis=3,
            tiled=True,
        ),
        "col",
        split_axis=2,
        concat_axis=2,
        tiled=True,
    )
    restored = jnp.take(returned, phys_device, axis=2).reshape(fields, local_levels, local_cols)
    sunlit_heating = heat_blocks.reshape(levels, columns // 2).astype(jnp.bfloat16)
    return (restored, sunlit_heating)


def solution(mesh):
    return jax.shard_map(
        local,
        mesh=mesh,
        in_specs=(P(None, "lev", "col"), P(), P(), P(), P(), P(), P("col"), P("col")),
        out_specs=(P(None, "lev", "col"), P(None, ("col", "lev"))),
        check_vma=False,
    )
```

profile of v0, /device:TPU:1, one launch (start us, length us, event | category | flops | bytes accessed | tf_op | source)
XLA Modules:
  0.0 135.9 jit_solution(9026844451925080249)
XLA Ops:
  0.6 0.0 copy-start
  0.6 0.9 select_reduce_fusion
  1.5 1.6 %gather_fusion = s32[128]{0:T(128)S(1)} fusion(s32[128]{0:T(128)} %param.17, s32[1024]{0:T(1024)S(1)} %pad_clamp_fusion.2), kind=kCustom, calls=%fused_computation.2 | custom fusion | bytes 1536 | tf_op jit(solution)/shard_map/jit(_take)/gather | solution.py:50
  3.1 0.8 broadcast_in_dim.43
  4.0 18.4 %all-to-all-start.2 = ((s32[1,1,128,4]{3,1,0,2:T(1,128)}), s32[1,1,128,4]{3,1,0,2:T(1,128)S(1)}, u32[]{:S(2)}, u32[]{:S(2)}) async-start(s32[1,1,128,4]{3,1,0,2:T(1,128)} %broadcast_in_dim.43), calls=%async_computation.2 | async-start | bytes 131072 | tf_op jit(solution)/shard_map/all_to_all | solution.py:62
  22.4 2.3 %copy.43 = bf16[10,32,512]{1,2,0:T(8,128)(2,1)} copy(bf16[10,32,512]{2,1,0:T(8,128)(2,1)} %param.10) | data formatting | bytes 655360 | tf_op args[0]
  24.7 3.5 %gather_fusion.2 = bf16[128,10,32,4]{2,3,1,0:T(4,128)(2,1)S(1)} fusion(bf16[10,32,128,4]{1,3,2,0:T(4,128)(2,1)} %bitcast.64, s32[1024]{0:T(1024)S(1)} %pad_clamp_fusion.3), kind=kCustom, calls=%fused_computation.clone | custom fusion | bytes 655872 | tf_op jit(solution)/shard_map/jit(_take)/gather | solution.py:51
  28.2 1.8 %fusion.11 = bf16[128,10,4,32]{3,2,1,0:T(4,128)(2,1)} fusion(bf16[128,10,32,4]{2,3,1,0:T(4,128)(2,1)S(1)} %gather_fusion.2, pred[128]{0:T(512)(128)(4,1)S(1)} %get-tuple-element.16), kind=kLoop, calls=%fused_computation.38 | loop fusion | flops 163840 | bytes 655488
  30.0 3.5 %reshape.133 = bf16[128,2,640]{2,1,0:T(2,128)(2,1)} reshape(bf16[128,10,4,32]{3,2,1,0:T(4,128)(2,1)} %fusion.11) | data formatting | bytes 655360
  33.5 0.3 all-to-all-done.2
  33.8 13.5 %all-to-all-start = ((bf16[128,2,640]{2,1,0:T(2,128)(2,1)}), bf16[128,2,640]{2,1,0:T(2,128)(2,1)S(1)}, u32[]{:S(2)}, u32[]{:S(2)}) async-start(bf16[128,2,640]{2,1,0:T(2,128)(2,1)} %reshape.133), calls=%async_computation | async-start | bytes 655360 | tf_op jit(solution)/shard_map/all_to_all | solution.py:55
  47.3 0.7 copy.48
  47.9 15.9 %all-to-all-done = bf16[128,2,640]{2,1,0:T(2,128)(2,1)S(1)} async-done(((bf16[128,2,640]{2,1,0:T(2,128)(2,1)}), bf16[128,2,640]{2,1,0:T(2,128)(2,1)S(1)}, u32[]{:S(2)}, u32[]{:S(2)}) %all-to-all-start) | async-done | bytes 327712 | tf_op jit(solution)/shard_map/all_to_all | solution.py:55
  63.9 4.0 %all-to-all-start.3 = ((s32[1,1,128,4]{2,1,0,3:T(1,128)}), s32[1,1,128,4]{2,1,0,3:T(1,128)S(1)}, u32[]{:S(2)}, u32[]{:S(2)}) async-start(s32[1,1,128,4]{2,1,0,3:T(1,128)} %copy.48), calls=%async_computation.3 | async-start | bytes 4096 | tf_op jit(solution)/shard_map/all_to_all | solution.py:61
  67.9 0.6 reshape.134
  68.5 0.0 copy-start.2
  68.5 1.4 %copy.44 = bf16[10,32,128,4]{2,1,0,3:T(8,128)(2,1)} copy(bf16[10,32,128,4]{1,3,0,2:T(4,128)(2,1)S(1)} %bitcast.65) | data formatting | bytes 655360 | tf_op jit(solution)/shard_map/all_to_all | solution.py:55
  69.9 2.0 %all-to-all-done.3 = s32[1,1,128,4]{2,1,0,3:T(1,128)S(1)} async-done(((s32[1,1,128,4]{2,1,0,3:T(1,128)}), s32[1,1,128,4]{2,1,0,3:T(1,128)S(1)}, u32[]{:S(2)}, u32[]{:S(2)}) %all-to-all-start.3) | async-done | bytes 2080 | tf_op jit(solution)/shard_map/all_to_all | solution.py:61
  71.9 3.5 %all-to-all-start.1 = ((bf16[10,32,128,4]{2,1,0,3:T(8,128)(2,1)}), bf16[10,32,128,4]{2,1,0,3:T(8,128)(2,1)S(1)}, u32[]{:S(2)}, u32[]{:S(2)}) async-start(bf16[10,32,128,4]{2,1,0,3:T(8,128)(2,1)} %copy.44), calls=%async_computation.1 | async-start | bytes 655360 | tf_op jit(solution)/shard_map/all_to_all | solution.py:54
  75.4 0.1 pad.2.clone
  75.5 5.8 %all-to-all-done.1 = bf16[10,32,128,4]{2,1,0,3:T(8,128)(2,1)S(1)} async-done(((bf16[10,32,128,4]{2,1,0,3:T(8,128)(2,1)}), bf16[10,32,128,4]{2,1,0,3:T(8,128)(2,1)S(1)}, u32[]{:S(2)}, u32[]{:S(2)}) %all-to-all-start.1) | async-done | bytes 327712 | tf_op jit(solution)/shard_map/all_to_all | solution.py:54
  81.2 0.0 copy-start.1
  81.3 0.0 copy-start.3
  81.3 0.0 copy-done
  81.3 0.5 fusion.6
  81.8 0.1 copy.47
  81.9 0.1 copy.49
  82.0 0.6 copy-done.1
  82.6 0.5 fusion.8
  83.1 0.1 multiply_bitcast_fusion
  83.2 0.0 copy-start.4
  83.2 1.3 fusion.2
  84.5 1.2 copy.50
  85.7 3.6 %all-to-all-start.4 = ((bf16[10,128,128,1]{2,0,3,1:T(8,128)(2,1)}), bf16[10,128,128,1]{2,0,3,1:T(8,128)(2,1)S(1)}, u32[]{:S(2)}, u32[]{:S(2)}) async-start(bf16[10,128,128,1]{2,0,3,1:T(8,128)(2,1)} %copy.50), calls=%async_computation.4 | async-start | bytes 1048576 | tf_op jit(solution)/shard_map/all_to_all | solution.py:79
  89.4 6.7 %all-to-all-done.4 = bf16[10,128,128,1]{2,0,3,1:T(8,128)(2,1)S(1)} async-done(((bf16[10,128,128,1]{2,0,3,1:T(8,128)(2,1)}), bf16[10,128,128,1]{2,0,3,1:T(8,128)(2,1)S(1)}, u32[]{:S(2)}, u32[]{:S(2)}) %all-to-all-start.4) | async-done | bytes 327712 | tf_op jit(solution)/shard_map/all_to_all | solution.py:79
  96.1 3.6 %copy.52 = bf16[10,32,128,4]{1,3,0,2:T(4,128)(2,1)S(1)} copy(bf16[10,32,128,4]{2,0,1,3:T(8,128)(2,1)S(1)} %bitcast.72) | data formatting | bytes 655360 | tf_op jit(solution)/shard_map/all_to_all | solution.py:79
  99.7 2.1 %reshape.135 = bf16[128,2,640]{2,1,0:T(2,128)(2,1)} reshape(bf16[128,10,4,32]{3,2,1,0:T(4,128)(2,1)S(1)} %bitcast.66) | data formatting | bytes 655360
  101.8 9.2 %all-to-all-start.5 = ((bf16[128,2,640]{2,1,0:T(2,128)(2,1)}), bf16[128,2,640]{2,1,0:T(2,128)(2,1)S(1)}, u32[]{:S(2)}, u32[]{:S(2)}) async-start(bf16[128,2,640]{2,1,0:T(2,128)(2,1)} %reshape.135), calls=%async_computation.5 | async-start | bytes 655360 | tf_op jit(solution)/shard_map/all_to_all | solution.py:78
  111.0 2.5 %sort.17 = (s32[128]{0:T(128)}, s32[128]{0:T(128)S(1)}) sort(s32[128]{0:T(128)S(1)} %get-tuple-element.17, s32[128]{0:T(128)S(1)} %iota.11), dimensions={0}, to_apply=%region_1.0 | sort | flops 896 | bytes 2048 | tf_op jit(solution)/shard_map/jit(argsort)/sort | solution.py:72
  113.6 0.6 gather_fusion.1
  114.2 0.7 fusion.9
  114.9 12.8 %all-to-all-done.5 = bf16[128,2,640]{2,1,0:T(2,128)(2,1)S(1)} async-done(((bf16[128,2,640]{2,1,0:T(2,128)(2,1)}), bf16[128,2,640]{2,1,0:T(2,128)(2,1)S(1)}, u32[]{:S(2)}, u32[]{:S(2)}) %all-to-all-start.5) | async-done | bytes 327712 | tf_op jit(solution)/shard_map/all_to_all | solution.py:78
  127.7 0.6 reshape.136
  128.3 1.6 %copy.53 = bf16[10,32,128,4]{1,3,2,0:T(4,128)(2,1)} copy(bf16[10,32,128,4]{1,3,0,2:T(4,128)(2,1)S(1)} %bitcast.67) | data formatting | bytes 655360 | tf_op jit(solution)/shard_map/all_to_all | solution.py:78
  129.9 3.5 %gather_fusion.3 = bf16[128,10,32,4]{2,3,1,0:T(4,128)(2,1)S(1)} fusion(bf16[10,32,128,4]{1,3,2,0:T(4,128)(2,1)} %copy.53, s32[1024]{0:T(1024)S(1)} %pad_clamp_fusion.1), kind=kCustom, calls=%fused_computation.1.clone | custom fusion | bytes 655872 | tf_op jit(solution)/shard_map/jit(_take)/gather | solution.py:91
  133.5 0.7 select_bitcast_fusion
  134.2 0.5 copy.54
  134.7 1.2 copy.55
  (16 shorter events, 0.1 us)
Async XLA Ops:
  0.6 80.6 %copy-start = (bf16[1280,512]{1,0:T(8,128)(2,1)S(1)}, bf16[1280,512]{1,0:T(8,128)(2,1)}, u32[]{:S(2)}) copy-start(bf16[1280,512]{1,0:T(8,128)(2,1)} %param.12) | copy-start | bytes 3932164
  4.0 29.9 %all-to-all-start.2 = ((s32[1,1,128,4]{3,1,0,2:T(1,128)}), s32[1,1,128,4]{3,1,0,2:T(1,128)S(1)}, u32[]{:S(2)}, u32[]{:S(2)}) async-start(s32[1,1,128,4]{3,1,0,2:T(1,128)} %broadcast_in_dim.43), calls=%async_computation.2 | async-start | bytes 131072 | tf_op jit(solution)/shard_map/all_to_all | solution.py:62
  33.8 30.0 %all-to-all-start = ((bf16[128,2,640]{2,1,0:T(2,128)(2,1)}), bf16[128,2,640]{2,1,0:T(2,128)(2,1)S(1)}, u32[]{:S(2)}, u32[]{:S(2)}) async-start(bf16[128,2,640]{2,1,0:T(2,128)(2,1)} %reshape.133), calls=%async_computation | async-start | bytes 655360 | tf_op jit(solution)/shard_map/all_to_all | solution.py:55
  63.9 8.0 %all-to-all-start.3 = ((s32[1,1,128,4]{2,1,0,3:T(1,128)}), s32[1,1,128,4]{2,1,0,3:T(1,128)S(1)}, u32[]{:S(2)}, u32[]{:S(2)}) async-start(s32[1,1,128,4]{2,1,0,3:T(1,128)} %copy.48), calls=%async_computation.3 | async-start | bytes 4096 | tf_op jit(solution)/shard_map/all_to_all | solution.py:61
  68.5 12.8 %copy-start.2 = (bf16[512,256]{1,0:T(8,128)(2,1)S(1)}, bf16[512,256]{1,0:T(8,128)(2,1)}, u32[]{:S(2)}) copy-start(bf16[512,256]{1,0:T(8,128)(2,1)} %param.13) | copy-start | bytes 786436
  71.9 9.3 %all-to-all-start.1 = ((bf16[10,32,128,4]{2,1,0,3:T(8,128)(2,1)}), bf16[10,32,128,4]{2,1,0,3:T(8,128)(2,1)S(1)}, u32[]{:S(2)}, u32[]{:S(2)}) async-start(bf16[10,32,128,4]{2,1,0,3:T(8,128)(2,1)} %copy.44), calls=%async_computation.1 | async-start | bytes 655360 | tf_op jit(solution)/shard_map/all_to_all | solution.py:54
  81.2 1.3 copy-start.1
  81.3 1.3 copy-start.3
  83.2 6.2 %copy-start.4 = (s32[128]{0:T(128)S(1)}, s32[128]{0:T(128)}, u32[]{:S(2)}) copy-start(s32[128]{0:T(128)} %param.16) | copy-start | bytes 1540
  85.7 10.4 %all-to-all-start.4 = ((bf16[10,128,128,1]{2,0,3,1:T(8,128)(2,1)}), bf16[10,128,128,1]{2,0,3,1:T(8,128)(2,1)S(1)}, u32[]{:S(2)}, u32[]{:S(2)}) async-start(bf16[10,128,128,1]{2,0,3,1:T(8,128)(2,1)} %copy.50), calls=%async_computation.4 | async-start | bytes 1048576 | tf_op jit(solution)/shard_map/all_to_all | solution.py:79
  101.8 25.9 %all-to-all-start.5 = ((bf16[128,2,640]{2,1,0:T(2,128)(2,1)}), bf16[128,2,640]{2,1,0:T(2,128)(2,1)S(1)}, u32[]{:S(2)}, u32[]{:S(2)}) async-start(bf16[128,2,640]{2,1,0:T(2,128)(2,1)} %reshape.135), calls=%async_computation.5 | async-start | bytes 655360 | tf_op jit(solution)/shard_map/all_to_all | solution.py:78
where the time goes:
time: 137 us; the launch traced here: 136 us
  starting transfers between devices  52.2 us (38%)
  waiting for transfers between devices  43.4 us (32%)
  local copies, waits for them, and re-layouts  30.4 us (22%)
  other arithmetic  6.68 us (5%)
  matrix products  2.36 us (2%)
    all_to_all x1, starting transfers between devices, local(): lax.all_to_all(flag_tiles, 'col', split_axis=2, concat_axis=2, tiled=True)  18.4 us
    all_to_all x1, waiting for transfers between devices, local(): lax.all_to_all(grouped, 'col', split_axis=2, concat_axis=2, tiled=True)  15.9 us
    all_to_all x1, starting transfers between devices, local(): lax.all_to_all(grouped, 'col', split_axis=2, concat_axis=2, tiled=True)  13.5 us
    all_to_all x1, waiting for transfers between devices, local(): lax.all_to_all(lax.all_to_all(tendency.reshape(fields, levels, blocks, qu...  12.8 us
    unnamed x16, local copies, waits for them, and re-layouts  10.9 us
    all_to_all x1, starting transfers between devices, local(): lax.all_to_all(lax.all_to_all(tendency.reshape(fields, levels, blocks, qu...  9.2 us
    all_to_all x1, waiting for transfers between devices, local(): lax.all_to_all(tendency.reshape(fields, levels, blocks, quarter), 'lev',...  6.68 us
    all_to_all x1, waiting for transfers between devices, local(): lax.all_to_all(lax.all_to_all(grouped, 'col', split_axis=2, concat_axis=2...  5.76 us
  transfers between devices with their start and end apart: 6, of which 6 were waited for; matrix products, arithmetic and copies ran while one was open for 13% of the time, Pallas kernels for 0%

commit v1 on v0

v1 whole, which is shorter than its diff:
```python
import functools

import jax
import jax.numpy as jnp
from jax import lax
from jax.experimental import pallas as pl
from jax.experimental.pallas import tpu as pltpu
from jax.sharding import PartitionSpec as P

F32 = jnp.float32
BF16 = jnp.bfloat16
DARK = 2.0**100
GROUP = 4
WIDE = 384


def matmul(a, b, contract=((1,), (0,))):
    return lax.dot_general(a, b, (contract, ((), ())), preferred_element_type=F32)


def iota(shape, dim):
    return lax.broadcasted_iota(jnp.int32, shape, dim)


def onehot(mask):
    return jnp.where(mask, 1.0, 0.0).astype(BF16)


def per_column(row, blocks, block_cols):
    cols = blocks * block_cols
    spread = onehot(iota((blocks, cols), 1) // block_cols == iota((blocks, cols), 0))
    rows = jnp.broadcast_to(row.astype(F32), (16, blocks)).astype(BF16)
    return matmul(rows, spread)


def pack_kernel(state_ref, phys_ref, lit_ref, out_ref):
    rows, cols = state_ref.shape
    blocks = phys_ref.shape[1]
    block_cols = cols // blocks
    slots = blocks // GROUP
    dest = per_column(phys_ref[...], blocks, block_cols)[0:1].astype(jnp.int32)
    lit = per_column(lit_ref[...], blocks, block_cols)[0:1]
    place = ((dest % GROUP) * block_cols + iota((1, cols), 1) % block_cols) * slots + dest // GROUP
    sort = onehot(iota((cols, cols), 0) == place)
    flags = jnp.broadcast_to(lit, (WIDE - rows, cols)).astype(BF16)
    data = jnp.concatenate([state_ref[...], flags], axis=0)
    out_ref[...] = matmul(sort, data, ((1,), (1,))).astype(BF16)


def heat_kernel(got_ref, win_ref, wout_ref, out_ref):
    pieces, slots, _ = got_ref.shape
    levs = pieces // GROUP
    fields, levels, neurons = win_ref.shape
    part = levels // levs
    count = GROUP * slots
    total = None
    for lev in range(levs):
        cols = jnp.concatenate([got_ref[g * levs + lev] for g in range(GROUP)], axis=0)
        weight = win_ref[:, lev * part : (lev + 1) * part, :].reshape(fields * part, neurons)
        term = matmul(cols[:, : fields * part], weight)
        total = term if total is None else total + term
    lit = cols[:, fields * part : fields * part + 1].astype(F32)
    heat = matmul(jnp.tanh(total).astype(BF16), wout_ref[...])
    sent = jnp.where(lit > 0.5, heat, DARK).astype(BF16)
    row = iota((count, count), 0)
    order = onehot(iota((count, count), 1) == (row % GROUP) * slots + row // GROUP)
    out_ref[...] = matmul(order, sent).astype(BF16)


def pick_kernel(got_ref, out_ref):
    sources, levels = got_ref.shape
    picks = out_ref.shape[0]
    got = got_ref[...].astype(F32)
    lit = got < 0.5 * DARK
    heat = jnp.where(lit, got, 0.0).astype(BF16)
    lit_col = jnp.where(lit[:, :1], 1.0, 0.0)
    below = onehot(iota((sources, sources), 1) < iota((sources, sources), 0))
    rank = matmul(below, jnp.broadcast_to(lit_col, (sources, picks)).astype(BF16))
    choose = jnp.where(rank == iota((sources, picks), 1).astype(F32), lit_col, 0.0).astype(BF16)
    out_ref[...] = matmul(choose, heat, ((0,), (0,))).astype(BF16)


def tendency_kernel(
    lev_ref, x0, x1, x2, x3, coupling_ref, gin_ref, gout_ref, sin_ref, sout_ref, lit_ref, out_ref,
    whole, rows_ref,
):
    fields, part, cols = x0.shape
    levs = 4
    levels = part * levs
    blocks = lit_ref.shape[1]
    lev = lev_ref[0]
    for step, shard in enumerate((x0, x1, x2, x3)):
        source = lax.rem(lev + levs - step, levs)
        whole[:, pl.ds(pl.multiple_of(source * part, part), part), :] = shard[...]
    flat = whole[...].reshape(fields * levels, cols)
    hidden = jnp.tanh(matmul(flat, gin_ref[...], ((0,), (0,)))).astype(BF16)
    rows_ref[: 2 * levels] = matmul(gout_ref[...], hidden, ((0,), (1,)))
    hidden = jnp.tanh(matmul(flat, sin_ref[...], ((0,), (0,)))).astype(BF16)
    lit = per_column(lit_ref[...], blocks, cols // blocks)[0:1]
    rows_ref[2 * levels :] = matmul(sout_ref[...], hidden, ((0,), (1,))) * lit
    own = pl.multiple_of(lev * part, part)
    for field in range(fields):
        term = matmul(coupling_ref[field, pl.ds(own, part), :], whole[field])
        if field < 3:
            term = term + rows_ref[pl.ds(field * levels + own, part), :]
        out_ref[field] = term.astype(BF16)


def call(kernel, out, cost, scratch=(), smem=0, vmem=None, n_in=0):
    specs = [pl.BlockSpec(memory_space=pltpu.SMEM)] * smem
    specs += [pl.BlockSpec(memory_space=pltpu.VMEM)] * (n_in - smem)
    return pl.pallas_call(
        kernel,
        out_shape=jax.ShapeDtypeStruct(*out),
        in_specs=specs,
        out_specs=pl.BlockSpec(memory_space=pltpu.VMEM),
        scratch_shapes=list(scratch),
        cost_estimate=pl.CostEstimate(flops=cost[0], bytes_accessed=cost[1], transcendentals=0),
        compiler_params=pltpu.CompilerParams(vmem_limit_bytes=vmem or (24 << 20)),
    )


def local(state, level_coupling, gwd_in, gwd_out, sw_in, sw_out, phys_device, sunlit):
    fields, part, cols = state.shape
    blocks = phys_device.shape[0]
    levs = lax.axis_size("lev")
    col_count = lax.axis_size("col")
    levels = part * levs
    slots = blocks // GROUP
    members = GROUP * levs
    phys_row = phys_device.reshape(1, blocks)
    lit_row = sunlit.reshape(1, blocks)

    packed = call(pack_kernel, ((cols, WIDE), BF16), (2 * cols * cols * WIDE, 1 << 20), n_in=3)(
        state.reshape(fields * part, cols), phys_row, lit_row
    ).reshape(members, slots, WIDE)
    near = [[e * members + i for i in range(members)] for e in range(col_count // GROUP)]
    got = lax.all_to_all(packed, ("col", "lev"), 0, 0, tiled=True, axis_index_groups=near)

    shards = [state] + [
        lax.ppermute(state, "lev", [(i, (i + k) % levs) for i in range(levs)]) for k in (1, 2, 3)
    ]

    heat = call(
        heat_kernel, ((slots * GROUP, levels), BF16),
        (2 * blocks * (fields * levels * 512 + 512 * levels), 2 << 20), n_in=3,
    )(got, sw_in.reshape(fields, levels, -1), sw_out)
    far = [[e * GROUP + g for e in range(col_count // GROUP)] for g in range(GROUP)]
    arrived = lax.all_to_all(
        heat.reshape(slots, GROUP, levels), "col", 0, 0, tiled=True, axis_index_groups=far
    ).reshape(col_count, levels)

    lev = lax.axis_index("lev").astype(jnp.int32).reshape(1)
    tendency = call(
        tendency_kernel, ((fields, part, cols), BF16),
        (2 * cols * (fields * levels * 1024 + 512 * 3 * levels), 5 << 20),
        scratch=[pltpu.VMEM((fields, levels, cols), BF16), pltpu.VMEM((3 * levels, cols), F32)],
        smem=1, n_in=11,
    )(lev, *shards, level_coupling, gwd_in, gwd_out, sw_in, sw_out, lit_row)

    picked = call(pick_kernel, ((blocks // 2, levels), BF16), (1 << 22, 1 << 16), n_in=1)(arrived)
    return tendency, picked.T


def solution(mesh):
    return jax.shard_map(
        local,
        mesh=mesh,
        in_specs=(P(None, "lev", "col"), P(), P(), P(), P(), P(), P("col"), P("col")),
        out_specs=(P(None, "lev", "col"), P(None, ("col", "lev"))),
        check_vma=False,
    )
```

time: 137 us -> 50.9 us (0.37)
  the two profiles are of different devices: /device:TPU:1 before, /device:TPU:2 now
where the time goes in v1:
time: 50.9 us; the launch traced here: 50.4 us
  starting transfers between devices  31.5 us (62%)
  Pallas kernels  7.75 us (15%)
  waiting for transfers between devices  6.11 us (12%)
  local copies, waits for them, and re-layouts  4.32 us (8%)
  between operations  0.78 us (2%)
    all_to_all x1, starting transfers between devices, local(): lax.all_to_all(heat.reshape(slots, GROUP, levels), 'col', 0, 0, tiled=Tru...  11.7 us
    ppermute x3, starting transfers between devices, local(): lax.ppermute(state, 'lev', [(i, (i + k) % levs) for i in range(levs)])  10.4 us
    all_to_all x1, starting transfers between devices, local(): lax.all_to_all(packed, ('col', 'lev'), 0, 0, tiled=True, axis_index_group...  9.38 us
    all_to_all x1, waiting for transfers between devices, local(): lax.all_to_all(heat.reshape(slots, GROUP, levels), 'col', 0, 0, tiled=Tru...  6.1 us
    unnamed x20, local copies, waits for them, and re-layouts  4.32 us
    pallas_call x1, Pallas kernels, local(): call(tendency_kernel, ((fields, part, cols), BF16), (2 * cols * (fields *...  4.11 us
    pallas_call x1, Pallas kernels, local(): call(pack_kernel, ((cols, WIDE), BF16), (2 * cols * cols * WIDE, 1 << 20)...  1.36 us
    pallas_call x1, Pallas kernels, local(): call(heat_kernel, ((slots * GROUP, levels), BF16), (2 * blocks * (fields...  1.29 us
  transfers between devices with their start and end apart: 5, of which 1 were waited for; matrix products, arithmetic and copies ran while one was open for 0% of the time, Pallas kernels for 11%

profile of v1, /device:TPU:2, one launch (start us, length us, event | category | flops | bytes accessed | tf_op | source)
XLA Modules:
  0.0 50.4 jit_solution(12023904077732091963)
XLA Ops:
  0.6 0.0 copy-start.1
  0.6 0.0 copy-start
  0.7 0.0 copy-start.3
  0.7 1.1 %copy-done.3 = bf16[10,32,512]{2,1,0:T(8,128)(2,1)S(1)} copy-done((bf16[10,32,512]{2,1,0:T(8,128)(2,1)S(1)}, bf16[10,32,512]{2,1,0:T(8,128)(2,1)}, u32[]{:S(2)}) %copy-start.3) | copy-done | bytes 327704
  1.7 0.0 copy-start.7
  1.7 0.7 %copy-done.7 = s32[128]{0:T(128)S(1)} copy-done((s32[128]{0:T(128)S(1)}, s32[128]{0:T(128)}, u32[]{:S(2)}) %copy-start.7) | copy-done | bytes 536
  2.4 0.0 copy-start.8
  2.4 0.7 %copy-done.8 = s32[128]{0:T(128)S(1)} copy-done((s32[128]{0:T(128)S(1)}, s32[128]{0:T(128)}, u32[]{:S(2)}) %copy-start.8) | copy-done | bytes 536
  3.0 1.4 %shard_map.96 = bf16[512,384]{1,0:T(8,128)(2,1)} custom-call(bf16[320,512]{1,0:T(8,128)(2,1)S(1)} %bitcast.11, s32[1,128]{1,0:T(1,128)S(1)} %bitcast.12, s32[1,128]{1,0:T(1,128)S(1)} %bitcast.13), custom_call_target="tpu_custom_call" | custom-call | flops 201326592 | bytes 1048576 | tf_op jit(solution)/shard_map/pallas_call | solution.py:134
  4.4 0.0 copy-start.2
  4.4 0.0 copy-start.4
  4.4 0.0 copy-start.9
  4.4 9.4 %all-to-all-start = ((bf16[16,32,384]{2,1,0:T(8,128)(2,1)}), bf16[16,32,384]{2,1,0:T(8,128)(2,1)S(1)}, u32[]{:S(2)}, u32[]{:S(2)}) async-start(bf16[16,32,384]{2,1,0:T(8,128)(2,1)} %bitcast.4), calls=%async_computation | async-start | bytes 786432 | tf_op jit(solution)/shard_map/all_to_all | solution.py:138
  13.8 2.1 %collective-permute-start.2 = (bf16[10,32,512]{2,1,0:T(8,128)(2,1)}, bf16[10,32,512]{2,1,0:T(8,128)(2,1)}, u32[]{:S(2)}, u32[]{:S(2)}) collective-permute-start(bf16[10,32,512]{2,1,0:T(8,128)(2,1)} %x0.1), channel_id=1, source_target_pairs={{0,3},{1,0},{2,1},{3,2},{4,7},{5,4},{6,5},{7,6},{8,11},{9,8},{10,9... | collective-permute-start | bytes 983048 | tf_op jit(solution)/shard_map/ppermute | solution.py:141
  15.9 4.6 %collective-permute-start.1 = (bf16[10,32,512]{2,1,0:T(8,128)(2,1)}, bf16[10,32,512]{2,1,0:T(8,128)(2,1)}, u32[]{:S(2)}, u32[]{:S(2)}) collective-permute-start(bf16[10,32,512]{2,1,0:T(8,128)(2,1)} %x0.1), channel_id=1, source_target_pairs={{0,2},{1,3},{2,0},{3,1},{4,6},{5,7},{6,4},{7,5},{8,10},{9,11},{10,... | collective-permute-start | bytes 983048 | tf_op jit(solution)/shard_map/ppermute | solution.py:141
  20.6 3.7 %collective-permute-start = (bf16[10,32,512]{2,1,0:T(8,128)(2,1)}, bf16[10,32,512]{2,1,0:T(8,128)(2,1)}, u32[]{:S(2)}, u32[]{:S(2)}) collective-permute-start(bf16[10,32,512]{2,1,0:T(8,128)(2,1)} %x0.1), channel_id=1, source_target_pairs={{0,1},{1,2},{2,3},{3,0},{4,5},{5,6},{6,7},{7,4},{8,9},{9,10},{10,1... | collective-permute-start | bytes 983048 | tf_op jit(solution)/shard_map/ppermute | solution.py:141
  24.3 0.0 all-to-all-done.got_ref
  24.3 0.0 copy-done.1
  24.3 0.0 copy-done
  24.3 1.3 %shard_map.97 = bf16[128,128]{1,0:T(8,128)(2,1)} custom-call(bf16[16,32,384]{2,1,0:T(8,128)(2,1)S(1)} %all-to-all-done.got_ref, bf16[10,128,512]{2,1,0:T(8,128)(2,1)S(1)} %bitcast.9, bf16[512,128]{1,0:T(8,128)(2,1)S(1)} %copy-done.1), custom_call_target="tpu_custom_call" | custom-call | flops 184549376 | bytes 2097152 | tf_op jit(solution)/shard_map/pallas_call | solution.py:144
  25.6 11.7 %all-to-all-start.1 = ((bf16[32,4,128]{2,1,0:T(4,128)(2,1)}), bf16[32,4,128]{2,1,0:T(4,128)(2,1)S(1)}, u32[]{:S(2)}, u32[]{:S(2)}) async-start(bf16[32,4,128]{2,1,0:T(4,128)(2,1)} %bitcast.6), calls=%async_computation.1 | async-start | bytes 65536 | tf_op jit(solution)/shard_map/all_to_all | solution.py:149
  37.3 0.0 collective-permute-done.2.x3
  37.3 0.0 collective-permute-done.1.x2
  37.3 0.0 collective-permute-done.x1
  37.3 0.0 copy-done.2
  37.3 0.0 copy-done.4
  37.3 0.0 copy-done.9
  37.3 0.0 copy-start.5
  37.3 1.0 %copy-done.5 = bf16[10,128,128]{2,1,0:T(8,128)(2,1)S(1)} copy-done((bf16[10,128,128]{2,1,0:T(8,128)(2,1)S(1)}, bf16[10,128,128]{2,1,0:T(8,128)(2,1)}, u32[]{:S(2)}) %copy-start.5) | copy-done | bytes 327704
  38.3 0.0 copy-start.6
  38.3 0.9 %copy-done.6 = bf16[512,256]{1,0:T(8,128)(2,1)S(1)} copy-done((bf16[512,256]{1,0:T(8,128)(2,1)S(1)}, bf16[512,256]{1,0:T(8,128)(2,1)}, u32[]{:S(2)}) %copy-start.6) | copy-done | bytes 262168
  39.2 4.1 %shard_map.95 = bf16[10,32,512]{2,1,0:T(8,128)(2,1)} custom-call(s32[1]{0:T(128)} %bitcast.lev_ref, bf16[10,32,512]{2,1,0:T(8,128)(2,1)S(1)} %copy-done.4, bf16[10,32,512]{2,1,0:T(8,128)(2,1)} %collective-permute-done.x1, bf16[10,32,512]{2,1,0:T(8,128)(2,1)} %collective-permute-done.1.x2, bf16[10,32,512]{2,1,0:T(8,128)(2,1)} %collective-permute-done.2.x3, ...), custom_call_target="tpu_custom_call" | custom-call | flops 1543503872 | bytes 5242880 | tf_op jit(solution)/shard_map/pallas_call | solution.py:154
  43.4 6.1 %all-to-all-done.1 = bf16[32,4,128]{2,1,0:T(4,128)(2,1)S(1)} async-done(((bf16[32,4,128]{2,1,0:T(4,128)(2,1)}), bf16[32,4,128]{2,1,0:T(4,128)(2,1)S(1)}, u32[]{:S(2)}, u32[]{:S(2)}) %all-to-all-start.1) | async-done | bytes 32800 | tf_op jit(solution)/shard_map/all_to_all | solution.py:149
  49.5 1.0 %shard_map.98 = bf16[64,128]{1,0:T(8,128)(2,1)} custom-call(bf16[128,128]{1,0:T(8,128)(2,1)S(1)} %bitcast.10), custom_call_target="tpu_custom_call" | custom-call | flops 4194304 | bytes 65536 | tf_op jit(solution)/shard_map/pallas_call | solution.py:161
Async XLA Ops:
  0.6 23.6 %copy-start.1 = (bf16[512,128]{1,0:T(8,128)(2,1)S(1)}, bf16[512,128]{1,0:T(8,128)(2,1)}, u32[]{:S(2)}) copy-start(bf16[512,128]{1,0:T(8,128)(2,1)} %wout_ref.1) | copy-start | bytes 393220
  0.6 23.6 %copy-start = (bf16[1280,512]{1,0:T(8,128)(2,1)S(1)}, bf16[1280,512]{1,0:T(8,128)(2,1)}, u32[]{:S(2)}) copy-start(bf16[1280,512]{1,0:T(8,128)(2,1)} %sin_ref.1) | copy-start | bytes 3932164
  0.7 1.1 %copy-start.3 = (bf16[10,32,512]{2,1,0:T(8,128)(2,1)S(1)}, bf16[10,32,512]{2,1,0:T(8,128)(2,1)}, u32[]{:S(2)}) copy-start(bf16[10,32,512]{2,1,0:T(8,128)(2,1)} %x0.1) | copy-start | bytes 983044
  1.7 0.7 %copy-start.7 = (s32[128]{0:T(128)S(1)}, s32[128]{0:T(128)}, u32[]{:S(2)}) copy-start(s32[128]{0:T(128)} %param.14) | copy-start | bytes 1540
  2.4 0.7 %copy-start.8 = (s32[128]{0:T(128)S(1)}, s32[128]{0:T(128)}, u32[]{:S(2)}) copy-start(s32[128]{0:T(128)} %param.15) | copy-start | bytes 1540
  4.4 32.9 %copy-start.2 = (bf16[1280,512]{1,0:T(8,128)(2,1)S(1)}, bf16[1280,512]{1,0:T(8,128)(2,1)}, u32[]{:S(2)}) copy-start(bf16[1280,512]{1,0:T(8,128)(2,1)} %gin_ref.1) | copy-start | bytes 3932164
  4.4 32.9 %copy-start.4 = (bf16[10,32,512]{2,1,0:T(8,128)(2,1)S(1)}, bf16[10,32,512]{2,1,0:T(8,128)(2,1)}, u32[]{:S(2)}) copy-start(bf16[10,32,512]{2,1,0:T(8,128)(2,1)} %x0.1) | copy-start | bytes 983044
  4.4 32.9 %copy-start.9 = (s32[128]{0:T(128)S(1)}, s32[128]{0:T(128)}, u32[]{:S(2)}) copy-start(s32[128]{0:T(128)} %param.15) | copy-start | bytes 1540
  4.4 19.8 %all-to-all-start = ((bf16[16,32,384]{2,1,0:T(8,128)(2,1)}), bf16[16,32,384]{2,1,0:T(8,128)(2,1)S(1)}, u32[]{:S(2)}, u32[]{:S(2)}) async-start(bf16[16,32,384]{2,1,0:T(8,128)(2,1)} %bitcast.4), calls=%async_computation | async-start | bytes 786432 | tf_op jit(solution)/shard_map/all_to_all | solution.py:138
  13.8 23.5 %collective-permute-start.2 = (bf16[10,32,512]{2,1,0:T(8,128)(2,1)}, bf16[10,32,512]{2,1,0:T(8,128)(2,1)}, u32[]{:S(2)}, u32[]{:S(2)}) collective-permute-start(bf16[10,32,512]{2,1,0:T(8,128)(2,1)} %x0.1), channel_id=1, source_target_pairs={{0,3},{1,0},{2,1},{3,2},{4,7},{5,4},{6,5},{7,6},{8,11},{9,8},{10,9... | collective-permute-start | bytes 983048 | tf_op jit(solution)/shard_map/ppermute | solution.py:141
  15.9 21.3 %collective-permute-start.1 = (bf16[10,32,512]{2,1,0:T(8,128)(2,1)}, bf16[10,32,512]{2,1,0:T(8,128)(2,1)}, u32[]{:S(2)}, u32[]{:S(2)}) collective-permute-start(bf16[10,32,512]{2,1,0:T(8,128)(2,1)} %x0.1), channel_id=1, source_target_pairs={{0,2},{1,3},{2,0},{3,1},{4,6},{5,7},{6,4},{7,5},{8,10},{9,11},{10,... | collective-permute-start | bytes 983048 | tf_op jit(solution)/shard_map/ppermute | solution.py:141
  20.6 16.7 %collective-permute-start = (bf16[10,32,512]{2,1,0:T(8,128)(2,1)}, bf16[10,32,512]{2,1,0:T(8,128)(2,1)}, u32[]{:S(2)}, u32[]{:S(2)}) collective-permute-start(bf16[10,32,512]{2,1,0:T(8,128)(2,1)} %x0.1), channel_id=1, source_target_pairs={{0,1},{1,2},{2,3},{3,0},{4,5},{5,6},{6,7},{7,4},{8,9},{9,10},{10,1... | collective-permute-start | bytes 983048 | tf_op jit(solution)/shard_map/ppermute | solution.py:141
  25.6 23.9 %all-to-all-start.1 = ((bf16[32,4,128]{2,1,0:T(4,128)(2,1)}), bf16[32,4,128]{2,1,0:T(4,128)(2,1)S(1)}, u32[]{:S(2)}, u32[]{:S(2)}) async-start(bf16[32,4,128]{2,1,0:T(4,128)(2,1)} %bitcast.6), calls=%async_computation.1 | async-start | bytes 65536 | tf_op jit(solution)/shard_map/all_to_all | solution.py:149
  37.3 1.0 %copy-start.5 = (bf16[10,128,128]{2,1,0:T(8,128)(2,1)S(1)}, bf16[10,128,128]{2,1,0:T(8,128)(2,1)}, u32[]{:S(2)}) copy-start(bf16[10,128,128]{2,1,0:T(8,128)(2,1)} %coupling_ref.1) | copy-start | bytes 983044
  38.3 0.9 %copy-start.6 = (bf16[512,256]{1,0:T(8,128)(2,1)S(1)}, bf16[512,256]{1,0:T(8,128)(2,1)}, u32[]{:S(2)}) copy-start(bf16[512,256]{1,0:T(8,128)(2,1)} %gout_ref.1) | copy-start | bytes 786436

commit v2 on v1

v2 whole, which is shorter than its diff:
```python
import jax
import jax.numpy as jnp
from jax import lax
from jax.experimental import pallas as pl
from jax.experimental.pallas import tpu as pltpu
from jax.sharding import PartitionSpec as P

F32 = jnp.float32
BF16 = jnp.bfloat16
DARK = 2.0**100
GROUP = 4
WIDE = 384
PIECES = 2


def matmul(a, b, contract=((1,), (0,))):
    return lax.dot_general(a, b, (contract, ((), ())), preferred_element_type=F32)


def iota(shape, dim):
    return lax.broadcasted_iota(jnp.int32, shape, dim)


def onehot(mask):
    return jnp.where(mask, 1.0, 0.0).astype(BF16)


def per_column(row, blocks, block_cols):
    cols = blocks * block_cols
    spread = onehot(iota((blocks, cols), 1) // block_cols == iota((blocks, cols), 0))
    rows = jnp.broadcast_to(row.astype(F32), (16, blocks)).astype(BF16)
    return matmul(rows, spread)


def pack_kernel(state_hbm, phys_hbm, lit_hbm, out_hbm, data, phys_row, lit_row, packed, sems):
    fields, part, cols = state_hbm.shape
    blocks = phys_row.shape[1]
    block_cols = cols // blocks
    slots = blocks // GROUP
    copies = [
        pltpu.make_async_copy(phys_hbm, phys_row, sems.at[0]),
        pltpu.make_async_copy(lit_hbm, lit_row, sems.at[1]),
        pltpu.make_async_copy(state_hbm, data.at[:fields], sems.at[2]),
    ]
    for copy in copies:
        copy.start()
    spread = onehot(iota((blocks, cols), 1) // block_cols == iota((blocks, cols), 0))
    column = iota((1, cols), 1) % block_cols
    copies[0].wait()
    copies[1].wait()
    both = jnp.where(iota((16, blocks), 0) == 0, phys_row[...], lit_row[...])
    both = matmul(both.astype(F32).astype(BF16), spread)
    dest = both[0:1].astype(jnp.int32)
    place = ((dest % GROUP) * block_cols + column) * slots + dest // GROUP
    data[fields:] = jnp.broadcast_to(both[1:2], (2, part, cols)).astype(BF16)
    piece = cols // PIECES
    sorts = [onehot(iota((piece, cols), 0) + c * piece == place) for c in range(PIECES)]
    copies[2].wait()
    flat = data[...].reshape(WIDE, cols)
    writes = []
    for c, sort in enumerate(sorts):
        rows_c = pl.ds(c * piece, piece)
        packed[rows_c] = matmul(sort, flat, ((1,), (1,))).astype(BF16)
        writes.append(pltpu.make_async_copy(packed.at[rows_c], out_hbm.at[rows_c], sems.at[3 + c]))
        writes[-1].start()
    for write in writes:
        write.wait()


def heat_kernel(got_ref, win_ref, wout_ref, out_ref):
    pieces, slots, _ = got_ref.shape
    levs = pieces // GROUP
    fields, levels, neurons = win_ref.shape
    part = levels // levs
    count = GROUP * slots
    total = None
    for lev in range(levs):
        cols = jnp.concatenate([got_ref[g * levs + lev] for g in range(GROUP)], axis=0)
        weight = win_ref[:, lev * part : (lev + 1) * part, :].reshape(fields * part, neurons)
        term = matmul(cols[:, : fields * part], weight)
        total = term if total is None else total + term
    lit = cols[:, fields * part : fields * part + 1].astype(F32)
    heat = matmul(jnp.tanh(total).astype(BF16), wout_ref[...])
    sent = jnp.where(lit > 0.5, heat, DARK).astype(BF16)
    row = iota((count, count), 0)
    order = onehot(iota((count, count), 1) == (row % GROUP) * slots + row // GROUP)
    out_ref[...] = matmul(order, sent).astype(BF16)


def pick_kernel(got_ref, out_ref):
    sources, levels = got_ref.shape
    picks = out_ref.shape[0]
    got = got_ref[...].astype(F32)
    lit = got < 0.5 * DARK
    heat = jnp.where(lit, got, 0.0).astype(BF16)
    lit_col = jnp.where(lit[:, :1], 1.0, 0.0)
    below = onehot(iota((sources, sources), 1) < iota((sources, sources), 0))
    rank = matmul(below, jnp.broadcast_to(lit_col, (sources, picks)).astype(BF16))
    choose = jnp.where(rank == iota((sources, picks), 1).astype(F32), lit_col, 0.0).astype(BF16)
    out_ref[...] = matmul(choose, heat, ((0,), (0,))).astype(BF16)


def tendency_kernel(
    lev_ref, x0, x1, x2, x3, coupling_hbm, gin_hbm, gout_hbm, sin_hbm, sout_hbm, lit_hbm, out_hbm,
    whole, coupling, gin, gout, sin, sout, lit_row, terms, drag, out, sems,
):
    fields, levels, cols = whole.shape
    part = out.shape[1]
    levs = levels // part
    blocks = lit_row.shape[1]
    lev = lev_ref[0]
    copies = []
    for step, shard in enumerate((x0, x1, x2, x3)):
        source = pl.multiple_of((lev ^ step) * part, part)
        copies.append(
            pltpu.make_async_copy(shard, whole.at[:, pl.ds(source, part), :], sems.at[step])
        )
    for source, target in (
        (coupling_hbm, coupling), (gin_hbm, gin), (gout_hbm, gout),
        (sin_hbm, sin), (sout_hbm, sout), (lit_hbm, lit_row),
    ):
        copies.append(pltpu.make_async_copy(source, target, sems.at[len(copies)]))
    for copy in copies:
        copy.start()
    own = pl.multiple_of(lev * part, part)
    for copy in copies[: levs + 1]:
        copy.wait()
    for field in range(fields):
        term = matmul(coupling[field, pl.ds(own, part), :], whole[field])
        if field < 3:
            terms[field] = term
        else:
            out[field] = term.astype(BF16)
    first = pltpu.make_async_copy(out.at[3:], out_hbm.at[3:], sems.at[len(copies)])
    first.start()
    flat = whole[...].reshape(fields * levels, cols)
    copies[levs + 1].wait()
    hidden = jnp.tanh(matmul(flat, gin[...], ((0,), (0,)))).astype(BF16)
    copies[levs + 2].wait()
    drag[: 2 * levels] = matmul(gout[...], hidden, ((0,), (1,)))
    copies[levs + 3].wait()
    hidden = jnp.tanh(matmul(flat, sin[...], ((0,), (0,)))).astype(BF16)
    copies[levs + 4].wait()
    copies[levs + 5].wait()
    lit = per_column(lit_row[...], blocks, cols // blocks)[0:1]
    drag[2 * levels :] = matmul(sout[...], hidden, ((0,), (1,))) * lit
    for field in range(3):
        added = drag[pl.ds(field * levels + own, part), :]
        out[field] = (terms[field] + added).astype(BF16)
    last = pltpu.make_async_copy(out.at[:3], out_hbm.at[:3], sems.at[len(copies) + 1])
    last.start()
    first.wait()
    last.wait()


def call(kernel, out, cost, spaces, scratch=(), vmem=24, result="v"):
    kinds = {"s": pltpu.SMEM, "v": pltpu.VMEM, "h": pltpu.HBM}
    return pl.pallas_call(
        kernel,
        out_shape=jax.ShapeDtypeStruct(*out),
        in_specs=[pl.BlockSpec(memory_space=kinds[space]) for space in spaces],
        out_specs=pl.BlockSpec(memory_space=kinds[result]),
        scratch_shapes=list(scratch),
        cost_estimate=pl.CostEstimate(flops=cost[0], bytes_accessed=cost[1], transcendentals=0),
        compiler_params=pltpu.CompilerParams(vmem_limit_bytes=vmem << 20),
    )


def local(state, level_coupling, gwd_in, gwd_out, sw_in, sw_out, phys_device, sunlit):
    fields, part, cols = state.shape
    blocks = phys_device.shape[0]
    levs = lax.axis_size("lev")
    col_count = lax.axis_size("col")
    levels = part * levs
    slots = blocks // GROUP
    members = GROUP * levs
    phys_row = phys_device.reshape(1, blocks)
    lit_row = sunlit.reshape(1, blocks)

    packed = call(
        pack_kernel, ((cols, WIDE), BF16), (2 * cols * cols * WIDE, 1 << 20), "hhh",
        [
            pltpu.VMEM((fields + 2, part, cols), BF16),
            pltpu.VMEM((1, blocks), jnp.int32),
            pltpu.VMEM((1, blocks), jnp.int32),
            pltpu.VMEM((cols, WIDE), BF16),
            pltpu.SemaphoreType.DMA((3 + PIECES,)),
        ],
        62, "h",
    )(state, phys_row, lit_row).reshape(members, slots, WIDE)
    near = [[e * members + i for i in range(members)] for e in range(col_count // GROUP)]
    got = lax.all_to_all(packed, ("col", "lev"), 0, 0, tiled=True, axis_index_groups=near)

    ring = [[(i, i ^ step) for i in range(levs)] for step in range(levs)]
    shards = [state] + [lax.ppermute(state, "lev", ring[step]) for step in range(1, levs)]

    heat = call(
        heat_kernel, ((slots * GROUP, levels), BF16),
        (2 * blocks * (fields * levels * 512 + 512 * levels), 2 << 20), "vvv",
    )(got, sw_in.reshape(fields, levels, -1), sw_out)
    far = [[e * GROUP + g for e in range(col_count // GROUP)] for g in range(GROUP)]
    arrived = lax.all_to_all(
        heat.reshape(slots, GROUP, levels), "col", 0, 0, tiled=True, axis_index_groups=far
    ).reshape(col_count, levels)

    lev = lax.axis_index("lev").astype(jnp.int32).reshape(1)
    tendency = call(
        tendency_kernel, ((fields, part, cols), BF16),
        (2 * cols * (fields * levels * 1024 + 512 * 3 * levels), 5 << 20), "s" + "h" * 10,
        [
            pltpu.VMEM((fields, levels, cols), BF16),
            pltpu.VMEM(level_coupling.shape, BF16),
            pltpu.VMEM(gwd_in.shape, BF16),
            pltpu.VMEM(gwd_out.shape, BF16),
            pltpu.VMEM(sw_in.shape, BF16),
            pltpu.VMEM(sw_out.shape, BF16),
            pltpu.VMEM((1, blocks), jnp.int32),
            pltpu.VMEM((3, part, cols), F32),
            pltpu.VMEM((3 * levels, cols), F32),
            pltpu.VMEM((fields, part, cols), BF16),
            pltpu.SemaphoreType.DMA((levs + 8,)),
        ],
        63, "h",
    )(lev, *shards, level_coupling, gwd_in, gwd_out, sw_in, sw_out, lit_row)

    picked = call(pick_kernel, ((blocks // 2, levels), BF16), (1 << 22, 1 << 16), "v")(arrived)
    return tendency, picked.T


def solution(mesh):
    return jax.shard_map(
        local,
        mesh=mesh,
        in_specs=(P(None, "lev", "col"), P(), P(), P(), P(), P(), P("col"), P("col")),
        out_specs=(P(None, "lev", "col"), P(None, ("col", "lev"))),
        check_vma=False,
    )
```

time: 50.9 us -> 48.6 us (0.955)
  local copies, waits for them, and re-layouts: 4.32 us -> 0.7 us
  Pallas kernels: 7.75 us -> 9.54 us
  starting transfers between devices: 31.5 us -> 30.8 us
    unnamed x20 -> x6, local copies, waits for them, and re-layouts: 4.32 us -> 0.7 us
    pallas_call x1, Pallas kernels: 1.36 us -> 2.28 us  [local(): call(pack_kernel, ((cols, WIDE), BF16), (2 * cols * cols * WIDE, 1 << 20)...]
    pallas_call x1, Pallas kernels: 4.11 us -> 4.98 us  [local(): call(tendency_kernel, ((fields, part, cols), BF16), (2 * cols * (fields *...]
    ppermute x3, starting transfers between devices: 10.4 us -> 9.81 us  [local(): lax.ppermute(state, 'lev', ring[step])]
  transfers between devices with their start and end apart: 5 -> 5, of which waited for: 1 -> 1; matrix products, arithmetic and copies ran while one was open for 0% -> 0% of each run, Pallas kernels for 11% -> 13%
where the time goes in v2:
time: 48.6 us; the launch traced here: 48.2 us
  starting transfers between devices  30.8 us (63%)
  Pallas kernels  9.54 us (20%)
  waiting for transfers between devices  6.5 us (13%)
  between operations  0.75 us (2%)
  local copies, waits for them, and re-layouts  0.7 us (1%)
    all_to_all x1, starting transfers between devices, local(): lax.all_to_all(heat.reshape(slots, GROUP, levels), 'col', 0, 0, tiled=Tru...  11.7 us
    ppermute x3, starting transfers between devices, local(): lax.ppermute(state, 'lev', ring[step])  9.81 us
    all_to_all x1, starting transfers between devices, local(): lax.all_to_all(packed, ('col', 'lev'), 0, 0, tiled=True, axis_index_group...  9.26 us
    all_to_all x1, waiting for transfers between devices, local(): lax.all_to_all(heat.reshape(slots, GROUP, levels), 'col', 0, 0, tiled=Tru...  6.48 us
    pallas_call x1, Pallas kernels, local(): call(tendency_kernel, ((fields, part, cols), BF16), (2 * cols * (fields *...  4.98 us
    pallas_call x1, Pallas kernels, local(): call(pack_kernel, ((cols, WIDE), BF16), (2 * cols * cols * WIDE, 1 << 20)...  2.28 us
    pallas_call x1, Pallas kernels, local(): call(heat_kernel, ((slots * GROUP, levels), BF16), (2 * blocks * (fields...  1.29 us
    pallas_call x1, Pallas kernels, local(): call(pick_kernel, ((blocks // 2, levels), BF16), (1 << 22, 1 << 16), 'v')  0.99 us
  transfers between devices with their start and end apart: 5, of which 1 were waited for; matrix products, arithmetic and copies ran while one was open for 0% of the time, Pallas kernels for 13%

profile of v2, /device:TPU:2, one launch (start us, length us, event | category | flops | bytes accessed | tf_op | source)
XLA Modules:
  0.0 48.2 jit_solution(14617608231353821316)
XLA Ops:
  0.6 0.0 copy-start.1
  0.6 0.0 copy-start
  0.7 2.3 %shard_map.96 = bf16[512,384]{1,0:T(8,128)(2,1)} custom-call(bf16[10,32,512]{2,1,0:T(8,128)(2,1)} %state_hbm.1, s32[1,128]{1,0:T(1,128)} %bitcast.12, s32[1,128]{1,0:T(1,128)} %bitcast.13), custom_call_target="tpu_custom_call" | custom-call | flops 201326592 | bytes 1048576 | tf_op jit(solution)/shard_map/pallas_call | solution.py:180
  2.9 9.3 %all-to-all-start = ((bf16[16,32,384]{2,1,0:T(8,128)(2,1)}), bf16[16,32,384]{2,1,0:T(8,128)(2,1)S(1)}, u32[]{:S(2)}, u32[]{:S(2)}) async-start(bf16[16,32,384]{2,1,0:T(8,128)(2,1)} %bitcast.10), calls=%async_computation | async-start | bytes 786432 | tf_op jit(solution)/shard_map/all_to_all | solution.py:192
  12.2 3.4 %collective-permute-start.2 = (bf16[10,32,512]{2,1,0:T(8,128)(2,1)}, bf16[10,32,512]{2,1,0:T(8,128)(2,1)S(1)}, u32[]{:S(2)}, u32[]{:S(2)}) collective-permute-start(bf16[10,32,512]{2,1,0:T(8,128)(2,1)} %state_hbm.1), channel_id=1, source_target_pairs={{0,3},{1,2},{2,1},{3,0},{4,7},{5,6},{6,5},{7,4},{8,11},{9,10},{10,... | collective-permute-start | bytes 983048 | tf_op jit(solution)/shard_map/ppermute | solution.py:195
  15.6 2.7 %collective-permute-start.1 = (bf16[10,32,512]{2,1,0:T(8,128)(2,1)}, bf16[10,32,512]{2,1,0:T(8,128)(2,1)}, u32[]{:S(2)}, u32[]{:S(2)}) collective-permute-start(bf16[10,32,512]{2,1,0:T(8,128)(2,1)} %state_hbm.1), channel_id=1, source_target_pairs={{0,2},{1,3},{2,0},{3,1},{4,6},{5,7},{6,4},{7,5},{8,10},{9,11},{10,... | collective-permute-start | bytes 983048 | tf_op jit(solution)/shard_map/ppermute | solution.py:195
  18.3 3.7 %collective-permute-start = (bf16[10,32,512]{2,1,0:T(8,128)(2,1)}, bf16[10,32,512]{2,1,0:T(8,128)(2,1)}, u32[]{:S(2)}, u32[]{:S(2)}) collective-permute-start(bf16[10,32,512]{2,1,0:T(8,128)(2,1)} %state_hbm.1), channel_id=1, source_target_pairs={{0,1},{1,0},{2,3},{3,2},{4,5},{5,4},{6,7},{7,6},{8,9},{9,8},{10,11... | collective-permute-start | bytes 983048 | tf_op jit(solution)/shard_map/ppermute | solution.py:195
  22.0 0.0 all-to-all-done.got_ref
  22.1 0.0 copy-done.1
  22.1 0.0 copy-done
  22.1 1.3 %shard_map.97 = bf16[128,128]{1,0:T(8,128)(2,1)} custom-call(bf16[16,32,384]{2,1,0:T(8,128)(2,1)S(1)} %all-to-all-done.got_ref, bf16[10,128,512]{2,1,0:T(8,128)(2,1)S(1)} %bitcast.8, bf16[512,128]{1,0:T(8,128)(2,1)S(1)} %copy-done.1), custom_call_target="tpu_custom_call" | custom-call | flops 184549376 | bytes 2097152 | tf_op jit(solution)/shard_map/pallas_call | solution.py:197
  23.4 11.7 %all-to-all-start.1 = ((bf16[32,4,128]{2,1,0:T(4,128)(2,1)}), bf16[32,4,128]{2,1,0:T(4,128)(2,1)S(1)}, u32[]{:S(2)}, u32[]{:S(2)}) async-start(bf16[32,4,128]{2,1,0:T(4,128)(2,1)} %bitcast.5), calls=%async_computation.1 | async-start | bytes 65536 | tf_op jit(solution)/shard_map/all_to_all | solution.py:202
  35.0 0.0 collective-permute-done.2.x3
  35.1 0.0 copy-start.2
  35.1 0.0 collective-permute-done.1.x2
  35.1 0.0 collective-permute-done.x1
  35.1 0.7 %copy-done.2 = bf16[10,32,512]{2,1,0:T(8,128)(2,1)} copy-done((bf16[10,32,512]{2,1,0:T(8,128)(2,1)}, bf16[10,32,512]{2,1,0:T(8,128)(2,1)S(1)}, u32[]{:S(2)}) %copy-start.2) | copy-done | bytes 327704
  35.8 5.0 %shard_map.95 = bf16[10,32,512]{2,1,0:T(8,128)(2,1)} custom-call(s32[1]{0:T(128)} %bitcast.lev_ref, bf16[10,32,512]{2,1,0:T(8,128)(2,1)} %state_hbm.1, bf16[10,32,512]{2,1,0:T(8,128)(2,1)} %collective-permute-done.x1, bf16[10,32,512]{2,1,0:T(8,128)(2,1)} %collective-permute-done.1.x2, bf16[10,32,512]{2,1,0:T(8,128)(2,1)} %copy-done.2, ...), custom_call_target="tpu_custom_call" | custom-call | flops 1543503872 | bytes 5242880 | tf_op jit(solution)/shard_map/pallas_call | solution.py:207
  40.8 6.5 %all-to-all-done.1 = bf16[32,4,128]{2,1,0:T(4,128)(2,1)S(1)} async-done(((bf16[32,4,128]{2,1,0:T(4,128)(2,1)}), bf16[32,4,128]{2,1,0:T(4,128)(2,1)S(1)}, u32[]{:S(2)}, u32[]{:S(2)}) %all-to-all-start.1) | async-done | bytes 32800 | tf_op jit(solution)/shard_map/all_to_all | solution.py:202
  47.2 1.0 %shard_map.98 = bf16[64,128]{1,0:T(8,128)(2,1)} custom-call(bf16[128,128]{1,0:T(8,128)(2,1)S(1)} %bitcast.9), custom_call_target="tpu_custom_call" | custom-call | flops 4194304 | bytes 65536 | tf_op jit(solution)/shard_map/pallas_call | solution.py:226
Async XLA Ops:
  0.6 21.4 %copy-start.1 = (bf16[512,128]{1,0:T(8,128)(2,1)S(1)}, bf16[512,128]{1,0:T(8,128)(2,1)}, u32[]{:S(2)}) copy-start(bf16[512,128]{1,0:T(8,128)(2,1)} %wout_ref.1) | copy-start | bytes 393220
  0.6 21.4 %copy-start = (bf16[1280,512]{1,0:T(8,128)(2,1)S(1)}, bf16[1280,512]{1,0:T(8,128)(2,1)}, u32[]{:S(2)}) copy-start(bf16[1280,512]{1,0:T(8,128)(2,1)} %sin_hbm.1) | copy-start | bytes 3932164
  2.9 19.1 %all-to-all-start = ((bf16[16,32,384]{2,1,0:T(8,128)(2,1)}), bf16[16,32,384]{2,1,0:T(8,128)(2,1)S(1)}, u32[]{:S(2)}, u32[]{:S(2)}) async-start(bf16[16,32,384]{2,1,0:T(8,128)(2,1)} %bitcast.10), calls=%async_computation | async-start | bytes 786432 | tf_op jit(solution)/shard_map/all_to_all | solution.py:192
  12.2 22.8 %collective-permute-start.2 = (bf16[10,32,512]{2,1,0:T(8,128)(2,1)}, bf16[10,32,512]{2,1,0:T(8,128)(2,1)S(1)}, u32[]{:S(2)}, u32[]{:S(2)}) collective-permute-start(bf16[10,32,512]{2,1,0:T(8,128)(2,1)} %state_hbm.1), channel_id=1, source_target_pairs={{0,3},{1,2},{2,1},{3,0},{4,7},{5,6},{6,5},{7,4},{8,11},{9,10},{10,... | collective-permute-start | bytes 983048 | tf_op jit(solution)/shard_map/ppermute | solution.py:195
  15.6 19.5 %collective-permute-start.1 = (bf16[10,32,512]{2,1,0:T(8,128)(2,1)}, bf16[10,32,512]{2,1,0:T(8,128)(2,1)}, u32[]{:S(2)}, u32[]{:S(2)}) collective-permute-start(bf16[10,32,512]{2,1,0:T(8,128)(2,1)} %state_hbm.1), channel_id=1, source_target_pairs={{0,2},{1,3},{2,0},{3,1},{4,6},{5,7},{6,4},{7,5},{8,10},{9,11},{10,... | collective-permute-start | bytes 983048 | tf_op jit(solution)/shard_map/ppermute | solution.py:195
  18.3 16.8 %collective-permute-start = (bf16[10,32,512]{2,1,0:T(8,128)(2,1)}, bf16[10,32,512]{2,1,0:T(8,128)(2,1)}, u32[]{:S(2)}, u32[]{:S(2)}) collective-permute-start(bf16[10,32,512]{2,1,0:T(8,128)(2,1)} %state_hbm.1), channel_id=1, source_target_pairs={{0,1},{1,0},{2,3},{3,2},{4,5},{5,4},{6,7},{7,6},{8,9},{9,8},{10,11... | collective-permute-start | bytes 983048 | tf_op jit(solution)/shard_map/ppermute | solution.py:195
  23.4 23.9 %all-to-all-start.1 = ((bf16[32,4,128]{2,1,0:T(4,128)(2,1)}), bf16[32,4,128]{2,1,0:T(4,128)(2,1)S(1)}, u32[]{:S(2)}, u32[]{:S(2)}) async-start(bf16[32,4,128]{2,1,0:T(4,128)(2,1)} %bitcast.5), calls=%async_computation.1 | async-start | bytes 65536 | tf_op jit(solution)/shard_map/all_to_all | solution.py:202
  35.1 0.7 %copy-start.2 = (bf16[10,32,512]{2,1,0:T(8,128)(2,1)}, bf16[10,32,512]{2,1,0:T(8,128)(2,1)S(1)}, u32[]{:S(2)}) copy-start(bf16[10,32,512]{2,1,0:T(8,128)(2,1)S(1)} %collective-permute-done.2.x3) | copy-start | bytes 983044

commit v3 on v2

--- a/solution.py
+++ b/solution.py
@@ -11,6 +11,7 @@
 GROUP = 4
 WIDE = 384
 PIECES = 2
+HEAD = 22
 
 
 def matmul(a, b, contract=((1,), (0,))):
@@ -83,18 +84,22 @@
     heat = matmul(jnp.tanh(total).astype(BF16), wout_ref[...])
     sent = jnp.where(lit > 0.5, heat, DARK).astype(BF16)
     row = iota((count, count), 0)
-    order = onehot(iota((count, count), 1) == (row % GROUP) * slots + row // GROUP)
+    slot = (row // GROUP + HEAD) % slots
+    order = onehot(iota((count, count), 1) == (row % GROUP) * slots + slot)
     out_ref[...] = matmul(order, sent).astype(BF16)
 
 
 def pick_kernel(got_ref, out_ref):
     sources, levels = got_ref.shape
+    row, col = iota((sources, sources), 0), iota((sources, sources), 1)
     picks = out_ref.shape[0]
     got = got_ref[...].astype(F32)
     lit = got < 0.5 * DARK
     heat = jnp.where(lit, got, 0.0).astype(BF16)
     lit_col = jnp.where(lit[:, :1], 1.0, 0.0)
-    below = onehot(iota((sources, sources), 1) < iota((sources, sources), 0))
+    turn = sources - HEAD * GROUP
+    place = [jnp.where(i < turn, i + HEAD * GROUP, i - turn) for i in (row, col)]
+    below = onehot(place[1] < place[0])
     rank = matmul(below, jnp.broadcast_to(lit_col, (sources, picks)).astype(BF16))
     choose = jnp.where(rank == iota((sources, picks), 1).astype(F32), lit_col, 0.0).astype(BF16)
     out_ref[...] = matmul(choose, heat, ((0,), (0,))).astype(BF16)
@@ -198,7 +203,7 @@
         heat_kernel, ((slots * GROUP, levels), BF16),
         (2 * blocks * (fields * levels * 512 + 512 * levels), 2 << 20), "vvv",
     )(got, sw_in.reshape(fields, levels, -1), sw_out)
-    far = [[e * GROUP + g for e in range(col_count // GROUP)] for g in range(GROUP)]
+    far = [[(e + HEAD) % slots * GROUP + g for e in range(slots)] for g in range(GROUP)]
     arrived = lax.all_to_all(
         heat.reshape(slots, GROUP, levels), "col", 0, 0, tiled=True, axis_index_groups=far
     ).reshape(col_count, levels)

time: 48.6 us -> 44.9 us (0.924)
  the two profiles are of different devices: /device:TPU:2 before, /device:TPU:1 now
where the time goes in v3:
time: 44.9 us; the launch traced here: 44.2 us
  starting transfers between devices  33.2 us (74%)
  Pallas kernels  9.54 us (21%)
  between operations  0.76 us (2%)
  local copies, waits for them, and re-layouts  0.7 us (2%)
    all_to_all x1, starting transfers between devices, local(): lax.all_to_all(heat.reshape(slots, GROUP, levels), 'col', 0, 0, tiled=Tru...  13.9 us
    all_to_all x1, starting transfers between devices, local(): lax.all_to_all(packed, ('col', 'lev'), 0, 0, tiled=True, axis_index_group...  10.3 us
    ppermute x3, starting transfers between devices, local(): lax.ppermute(state, 'lev', ring[step])  8.98 us
    pallas_call x1, Pallas kernels, local(): call(tendency_kernel, ((fields, part, cols), BF16), (2 * cols * (fields *...  4.99 us
    pallas_call x1, Pallas kernels, local(): call(pack_kernel, ((cols, WIDE), BF16), (2 * cols * cols * WIDE, 1 << 20)...  2.27 us
    pallas_call x1, Pallas kernels, local(): call(heat_kernel, ((slots * GROUP, levels), BF16), (2 * blocks * (fields...  1.29 us
    pallas_call x1, Pallas kernels, local(): call(pick_kernel, ((blocks // 2, levels), BF16), (1 << 22, 1 << 16), 'v')  0.99 us
  transfers between devices with their start and end apart: 5, of which 0 were waited for; matrix products, arithmetic and copies ran while one was open for 0% of the time, Pallas kernels for 14%

profile of v3, /device:TPU:1, one launch (start us, length us, event | category | flops | bytes accessed | tf_op | source)
XLA Modules:
  0.0 44.2 jit_solution(5617941813777438783)
XLA Ops:
  0.6 0.0 copy-start.1
  0.6 0.0 copy-start
  0.7 2.3 %shard_map.96 = bf16[512,384]{1,0:T(8,128)(2,1)} custom-call(bf16[10,32,512]{2,1,0:T(8,128)(2,1)} %state_hbm.1, s32[1,128]{1,0:T(1,128)} %bitcast.12, s32[1,128]{1,0:T(1,128)} %bitcast.13), custom_call_target="tpu_custom_call" | custom-call | flops 201326592 | bytes 1048576 | tf_op jit(solution)/shard_map/pallas_call | solution.py:185
  2.9 10.3 %all-to-all-start = ((bf16[16,32,384]{2,1,0:T(8,128)(2,1)}), bf16[16,32,384]{2,1,0:T(8,128)(2,1)S(1)}, u32[]{:S(2)}, u32[]{:S(2)}) async-start(bf16[16,32,384]{2,1,0:T(8,128)(2,1)} %bitcast.10), calls=%async_computation | async-start | bytes 786432 | tf_op jit(solution)/shard_map/all_to_all | solution.py:197
  13.2 4.5 %collective-permute-start.2 = (bf16[10,32,512]{2,1,0:T(8,128)(2,1)}, bf16[10,32,512]{2,1,0:T(8,128)(2,1)S(1)}, u32[]{:S(2)}, u32[]{:S(2)}) collective-permute-start(bf16[10,32,512]{2,1,0:T(8,128)(2,1)} %state_hbm.1), channel_id=1, source_target_pairs={{0,3},{1,2},{2,1},{3,0},{4,7},{5,6},{6,5},{7,4},{8,11},{9,10},{10,... | collective-permute-start | bytes 983048 | tf_op jit(solution)/shard_map/ppermute | solution.py:200
  17.7 2.5 %collective-permute-start.1 = (bf16[10,32,512]{2,1,0:T(8,128)(2,1)}, bf16[10,32,512]{2,1,0:T(8,128)(2,1)}, u32[]{:S(2)}, u32[]{:S(2)}) collective-permute-start(bf16[10,32,512]{2,1,0:T(8,128)(2,1)} %state_hbm.1), channel_id=1, source_target_pairs={{0,2},{1,3},{2,0},{3,1},{4,6},{5,7},{6,4},{7,5},{8,10},{9,11},{10,... | collective-permute-start | bytes 983048 | tf_op jit(solution)/shard_map/ppermute | solution.py:200
  20.2 2.0 %collective-permute-start = (bf16[10,32,512]{2,1,0:T(8,128)(2,1)}, bf16[10,32,512]{2,1,0:T(8,128)(2,1)}, u32[]{:S(2)}, u32[]{:S(2)}) collective-permute-start(bf16[10,32,512]{2,1,0:T(8,128)(2,1)} %state_hbm.1), channel_id=1, source_target_pairs={{0,1},{1,0},{2,3},{3,2},{4,5},{5,4},{6,7},{7,6},{8,9},{9,8},{10,11... | collective-permute-start | bytes 983048 | tf_op jit(solution)/shard_map/ppermute | solution.py:200
  22.2 0.0 all-to-all-done.got_ref
  22.2 0.0 copy-done.1
  22.2 0.0 copy-done
  22.2 1.3 %shard_map.97 = bf16[128,128]{1,0:T(8,128)(2,1)} custom-call(bf16[16,32,384]{2,1,0:T(8,128)(2,1)S(1)} %all-to-all-done.got_ref, bf16[10,128,512]{2,1,0:T(8,128)(2,1)S(1)} %bitcast.8, bf16[512,128]{1,0:T(8,128)(2,1)S(1)} %copy-done.1), custom_call_target="tpu_custom_call" | custom-call | flops 184549376 | bytes 2097152 | tf_op jit(solution)/shard_map/pallas_call | solution.py:202
  23.5 13.9 %all-to-all-start.1 = ((bf16[32,4,128]{2,1,0:T(4,128)(2,1)}), bf16[32,4,128]{2,1,0:T(4,128)(2,1)S(1)}, u32[]{:S(2)}, u32[]{:S(2)}) async-start(bf16[32,4,128]{2,1,0:T(4,128)(2,1)} %bitcast.5), calls=%async_computation.1 | async-start | bytes 65536 | tf_op jit(solution)/shard_map/all_to_all | solution.py:207
  37.4 0.0 collective-permute-done.2.x3
  37.5 0.0 copy-start.2
  37.5 0.0 collective-permute-done.1.x2
  37.5 0.0 collective-permute-done.x1
  37.5 0.7 %copy-done.2 = bf16[10,32,512]{2,1,0:T(8,128)(2,1)} copy-done((bf16[10,32,512]{2,1,0:T(8,128)(2,1)}, bf16[10,32,512]{2,1,0:T(8,128)(2,1)S(1)}, u32[]{:S(2)}) %copy-start.2) | copy-done | bytes 327704
  38.2 5.0 %shard_map.95 = bf16[10,32,512]{2,1,0:T(8,128)(2,1)} custom-call(s32[1]{0:T(128)} %bitcast.lev_ref, bf16[10,32,512]{2,1,0:T(8,128)(2,1)} %state_hbm.1, bf16[10,32,512]{2,1,0:T(8,128)(2,1)} %collective-permute-done.x1, bf16[10,32,512]{2,1,0:T(8,128)(2,1)} %collective-permute-done.1.x2, bf16[10,32,512]{2,1,0:T(8,128)(2,1)} %copy-done.2, ...), custom_call_target="tpu_custom_call" | custom-call | flops 1543503872 | bytes 5242880 | tf_op jit(solution)/shard_map/pallas_call | solution.py:212
  43.2 0.0 all-to-all-done.1
  43.2 1.0 %shard_map.98 = bf16[64,128]{1,0:T(8,128)(2,1)} custom-call(bf16[128,128]{1,0:T(8,128)(2,1)S(1)} %bitcast.9), custom_call_target="tpu_custom_call" | custom-call | flops 4194304 | bytes 65536 | tf_op jit(solution)/shard_map/pallas_call | solution.py:231
Async XLA Ops:
  0.6 21.6 %copy-start.1 = (bf16[512,128]{1,0:T(8,128)(2,1)S(1)}, bf16[512,128]{1,0:T(8,128)(2,1)}, u32[]{:S(2)}) copy-start(bf16[512,128]{1,0:T(8,128)(2,1)} %wout_ref.1) | copy-start | bytes 393220
  0.6 21.6 %copy-start = (bf16[1280,512]{1,0:T(8,128)(2,1)S(1)}, bf16[1280,512]{1,0:T(8,128)(2,1)}, u32[]{:S(2)}) copy-start(bf16[1280,512]{1,0:T(8,128)(2,1)} %sin_hbm.1) | copy-start | bytes 3932164
  2.9 19.3 %all-to-all-start = ((bf16[16,32,384]{2,1,0:T(8,128)(2,1)}), bf16[16,32,384]{2,1,0:T(8,128)(2,1)S(1)}, u32[]{:S(2)}, u32[]{:S(2)}) async-start(bf16[16,32,384]{2,1,0:T(8,128)(2,1)} %bitcast.10), calls=%async_computation | async-start | bytes 786432 | tf_op jit(solution)/shard_map/all_to_all | solution.py:197
  13.2 24.3 %collective-permute-start.2 = (bf16[10,32,512]{2,1,0:T(8,128)(2,1)}, bf16[10,32,512]{2,1,0:T(8,128)(2,1)S(1)}, u32[]{:S(2)}, u32[]{:S(2)}) collective-permute-start(bf16[10,32,512]{2,1,0:T(8,128)(2,1)} %state_hbm.1), channel_id=1, source_target_pairs={{0,3},{1,2},{2,1},{3,0},{4,7},{5,6},{6,5},{7,4},{8,11},{9,10},{10,... | collective-permute-start | bytes 983048 | tf_op jit(solution)/shard_map/ppermute | solution.py:200
  17.7 19.8 %collective-permute-start.1 = (bf16[10,32,512]{2,1,0:T(8,128)(2,1)}, bf16[10,32,512]{2,1,0:T(8,128)(2,1)}, u32[]{:S(2)}, u32[]{:S(2)}) collective-permute-start(bf16[10,32,512]{2,1,0:T(8,128)(2,1)} %state_hbm.1), channel_id=1, source_target_pairs={{0,2},{1,3},{2,0},{3,1},{4,6},{5,7},{6,4},{7,5},{8,10},{9,11},{10,... | collective-permute-start | bytes 983048 | tf_op jit(solution)/shard_map/ppermute | solution.py:200
  20.2 17.3 %collective-permute-start = (bf16[10,32,512]{2,1,0:T(8,128)(2,1)}, bf16[10,32,512]{2,1,0:T(8,128)(2,1)}, u32[]{:S(2)}, u32[]{:S(2)}) collective-permute-start(bf16[10,32,512]{2,1,0:T(8,128)(2,1)} %state_hbm.1), channel_id=1, source_target_pairs={{0,1},{1,0},{2,3},{3,2},{4,5},{5,4},{6,7},{7,6},{8,9},{9,8},{10,11... | collective-permute-start | bytes 983048 | tf_op jit(solution)/shard_map/ppermute | solution.py:200
  23.5 19.7 %all-to-all-start.1 = ((bf16[32,4,128]{2,1,0:T(4,128)(2,1)}), bf16[32,4,128]{2,1,0:T(4,128)(2,1)S(1)}, u32[]{:S(2)}, u32[]{:S(2)}) async-start(bf16[32,4,128]{2,1,0:T(4,128)(2,1)} %bitcast.5), calls=%async_computation.1 | async-start | bytes 65536 | tf_op jit(solution)/shard_map/all_to_all | solution.py:207
  37.5 0.7 %copy-start.2 = (bf16[10,32,512]{2,1,0:T(8,128)(2,1)}, bf16[10,32,512]{2,1,0:T(8,128)(2,1)S(1)}, u32[]{:S(2)}) copy-start(bf16[10,32,512]{2,1,0:T(8,128)(2,1)S(1)} %collective-permute-done.2.x3) | copy-start | bytes 983044

commit v4 on v3

--- a/solution.py
+++ b/solution.py
@@ -1,3 +1,5 @@
+import functools
+
 import jax
 import jax.numpy as jnp
 from jax import lax
@@ -11,7 +13,7 @@
 GROUP = 4
 WIDE = 384
 PIECES = 2
-HEAD = 22
+HEAD = 26
 
 
 def matmul(a, b, contract=((1,), (0,))):
@@ -106,8 +108,8 @@
 
 
 def tendency_kernel(
-    lev_ref, x0, x1, x2, x3, coupling_hbm, gin_hbm, gout_hbm, sin_hbm, sout_hbm, lit_hbm, out_hbm,
-    whole, coupling, gin, gout, sin, sout, lit_row, terms, drag, out, sems,
+    lev_ref, x0, x1, x2, x3, coupling_hbm, gin, gout_hbm, sin, sout, lit_hbm, out_hbm,
+    whole, coupling, gout, lit_row, terms, drag, out, sems,
 ):
     fields, levels, cols = whole.shape
     part = out.shape[1]
@@ -121,8 +123,7 @@
             pltpu.make_async_copy(shard, whole.at[:, pl.ds(source, part), :], sems.at[step])
         )
     for source, target in (
-        (coupling_hbm, coupling), (gin_hbm, gin), (gout_hbm, gout),
-        (sin_hbm, sin), (sout_hbm, sout), (lit_hbm, lit_row),
+        (coupling_hbm, coupling), (gout_hbm, gout), (lit_hbm, lit_row),
     ):
         copies.append(pltpu.make_async_copy(source, target, sems.at[len(copies)]))
     for copy in copies:
@@ -139,14 +140,11 @@
     first = pltpu.make_async_copy(out.at[3:], out_hbm.at[3:], sems.at[len(copies)])
     first.start()
     flat = whole[...].reshape(fields * levels, cols)
+    hidden = jnp.tanh(matmul(flat, gin[...], ((0,), (0,)))).astype(BF16)
     copies[levs + 1].wait()
-    hidden = jnp.tanh(matmul(flat, gin[...], ((0,), (0,)))).astype(BF16)
+    drag[: 2 * levels] = matmul(gout[...], hidden, ((0,), (1,)))
+    hidden = jnp.tanh(matmul(flat, sin[...], ((0,), (0,)))).astype(BF16)
     copies[levs + 2].wait()
-    drag[: 2 * levels] = matmul(gout[...], hidden, ((0,), (1,)))
-    copies[levs + 3].wait()
-    hidden = jnp.tanh(matmul(flat, sin[...], ((0,), (0,)))).astype(BF16)
-    copies[levs + 4].wait()
-    copies[levs + 5].wait()
     lit = per_column(lit_row[...], blocks, cols // blocks)[0:1]
     drag[2 * levels :] = matmul(sout[...], hidden, ((0,), (1,))) * lit
     for field in range(3):
@@ -167,7 +165,7 @@
         out_specs=pl.BlockSpec(memory_space=kinds[result]),
         scratch_shapes=list(scratch),
         cost_estimate=pl.CostEstimate(flops=cost[0], bytes_accessed=cost[1], transcendentals=0),
-        compiler_params=pltpu.CompilerParams(vmem_limit_bytes=vmem << 20),
+        compiler_params=pltpu.CompilerParams(vmem_limit_bytes=int(vmem * 1024) << 10),
     )
 
 
@@ -182,6 +180,7 @@
     phys_row = phys_device.reshape(1, blocks)
     lit_row = sunlit.reshape(1, blocks)
 
+    keep = functools.partial(pltpu.with_memory_space_constraint, memory_space=pltpu.HBM)
     packed = call(
         pack_kernel, ((cols, WIDE), BF16), (2 * cols * cols * WIDE, 1 << 20), "hhh",
         [
@@ -191,8 +190,8 @@
             pltpu.VMEM((cols, WIDE), BF16),
             pltpu.SemaphoreType.DMA((3 + PIECES,)),
         ],
-        62, "h",
-    )(state, phys_row, lit_row).reshape(members, slots, WIDE)
+        24, "h",
+    )(keep(state), keep(phys_row), keep(lit_row)).reshape(members, slots, WIDE)
     near = [[e * members + i for i in range(members)] for e in range(col_count // GROUP)]
     got = lax.all_to_all(packed, ("col", "lev"), 0, 0, tiled=True, axis_index_groups=near)
 
@@ -211,22 +210,19 @@
     lev = lax.axis_index("lev").astype(jnp.int32).reshape(1)
     tendency = call(
         tendency_kernel, ((fields, part, cols), BF16),
-        (2 * cols * (fields * levels * 1024 + 512 * 3 * levels), 5 << 20), "s" + "h" * 10,
+        (2 * cols * (fields * levels * 1024 + 512 * 3 * levels), 5 << 20), "shhhhhvhvvh",
         [
             pltpu.VMEM((fields, levels, cols), BF16),
             pltpu.VMEM(level_coupling.shape, BF16),
-            pltpu.VMEM(gwd_in.shape, BF16),
             pltpu.VMEM(gwd_out.shape, BF16),
-            pltpu.VMEM(sw_in.shape, BF16),
-            pltpu.VMEM(sw_out.shape, BF16),
             pltpu.VMEM((1, blocks), jnp.int32),
             pltpu.VMEM((3, part, cols), F32),
             pltpu.VMEM((3 * levels, cols), F32),
             pltpu.VMEM((fields, part, cols), BF16),
             pltpu.SemaphoreType.DMA((levs + 8,)),
         ],
-        63, "h",
-    )(lev, *shards, level_coupling, gwd_in, gwd_out, sw_in, sw_out, lit_row)
+        40, "h",
+    )(lev, *shards, keep(level_coupling), gwd_in, keep(gwd_out), sw_in, sw_out, keep(lit_row))
 
     picked = call(pick_kernel, ((blocks // 2, levels), BF16), (1 << 22, 1 << 16), "v")(arrived)
     return tendency, picked.T

time: 44.9 us -> 43.1 us (0.960)
  local copies, waits for them, and re-layouts: 0.7 us -> 0.02 us
  starting transfers between devices: 33.2 us -> 32.6 us
  Pallas kernels: 9.54 us -> 9.04 us
    all_to_all x1, starting transfers between devices: 13.9 us -> 13.2 us  [local(): lax.all_to_all(heat.reshape(slots, GROUP, levels), 'col', 0, 0, tiled=Tru...]
    unnamed x6 -> x8, local copies, waits for them, and re-layouts: 0.7 us -> 0.02 us
    pallas_call x1, Pallas kernels: 4.99 us -> 4.46 us  [local(): call(tendency_kernel, ((fields, part, cols), BF16), (2 * cols * (fields *...]
where the time goes in v4:
time: 43.1 us; the launch traced here: 42.4 us
  starting transfers between devices  32.6 us (76%)
  Pallas kernels  9.04 us (21%)
  between operations  0.79 us (2%)
    all_to_all x1, starting transfers between devices, local(): lax.all_to_all(heat.reshape(slots, GROUP, levels), 'col', 0, 0, tiled=Tru...  13.2 us
    all_to_all x1, starting transfers between devices, local(): lax.all_to_all(packed, ('col', 'lev'), 0, 0, tiled=True, axis_index_group...  10.4 us
    ppermute x3, starting transfers between devices, local(): lax.ppermute(state, 'lev', ring[step])  8.98 us
    pallas_call x1, Pallas kernels, local(): call(tendency_kernel, ((fields, part, cols), BF16), (2 * cols * (fields *...  4.46 us
    pallas_call x1, Pallas kernels, local(): call(pack_kernel, ((cols, WIDE), BF16), (2 * cols * cols * WIDE, 1 << 20)...  2.29 us
    pallas_call x1, Pallas kernels, local(): call(heat_kernel, ((slots * GROUP, levels), BF16), (2 * blocks * (fields...  1.3 us
    pallas_call x1, Pallas kernels, local(): call(pick_kernel, ((blocks // 2, levels), BF16), (1 << 22, 1 << 16), 'v')  0.99 us
  transfers between devices with their start and end apart: 5, of which 0 were waited for; matrix products, arithmetic and copies ran while one was open for 0% of the time, Pallas kernels for 14%

profile of v4, /device:TPU:1, one launch (start us, length us, event | category | flops | bytes accessed | tf_op | source)
XLA Modules:
  0.0 42.4 jit_solution(3572719876681913357)
XLA Ops:
  0.6 0.0 copy-start.1
  0.6 0.0 copy-start
  0.7 2.3 %shard_map.96 = bf16[512,384]{1,0:T(8,128)(2,1)} custom-call(bf16[10,32,512]{2,1,0:T(8,128)(2,1)} %state_hbm.1, s32[1,128]{1,0:T(1,128)} %bitcast.11, s32[1,128]{1,0:T(1,128)} %bitcast.12), custom_call_target="tpu_custom_call" | custom-call | flops 201326592 | bytes 1048576 | tf_op jit(solution)/shard_map/pallas_call | solution.py:184
  2.9 0.0 copy-start.2
  3.0 0.0 copy-start.3
  3.0 10.4 %all-to-all-start = ((bf16[16,32,384]{2,1,0:T(8,128)(2,1)}), bf16[16,32,384]{2,1,0:T(8,128)(2,1)S(1)}, u32[]{:S(2)}, u32[]{:S(2)}) async-start(bf16[16,32,384]{2,1,0:T(8,128)(2,1)} %bitcast.3), calls=%async_computation | async-start | bytes 786432 | tf_op jit(solution)/shard_map/all_to_all | solution.py:196
  13.4 4.5 %collective-permute-start.2 = (bf16[10,32,512]{2,1,0:T(8,128)(2,1)}, bf16[10,32,512]{2,1,0:T(8,128)(2,1)}, u32[]{:S(2)}, u32[]{:S(2)}) collective-permute-start(bf16[10,32,512]{2,1,0:T(8,128)(2,1)} %state_hbm.1), channel_id=1, source_target_pairs={{0,3},{1,2},{2,1},{3,0},{4,7},{5,6},{6,5},{7,4},{8,11},{9,10},{10,... | collective-permute-start | bytes 983048 | tf_op jit(solution)/shard_map/ppermute | solution.py:199
  17.9 2.5 %collective-permute-start.1 = (bf16[10,32,512]{2,1,0:T(8,128)(2,1)}, bf16[10,32,512]{2,1,0:T(8,128)(2,1)}, u32[]{:S(2)}, u32[]{:S(2)}) collective-permute-start(bf16[10,32,512]{2,1,0:T(8,128)(2,1)} %state_hbm.1), channel_id=1, source_target_pairs={{0,2},{1,3},{2,0},{3,1},{4,6},{5,7},{6,4},{7,5},{8,10},{9,11},{10,... | collective-permute-start | bytes 983048 | tf_op jit(solution)/shard_map/ppermute | solution.py:199
  20.3 2.0 %collective-permute-start = (bf16[10,32,512]{2,1,0:T(8,128)(2,1)}, bf16[10,32,512]{2,1,0:T(8,128)(2,1)}, u32[]{:S(2)}, u32[]{:S(2)}) collective-permute-start(bf16[10,32,512]{2,1,0:T(8,128)(2,1)} %state_hbm.1), channel_id=1, source_target_pairs={{0,1},{1,0},{2,3},{3,2},{4,5},{5,4},{6,7},{7,6},{8,9},{9,8},{10,11... | collective-permute-start | bytes 983048 | tf_op jit(solution)/shard_map/ppermute | solution.py:199
  22.4 0.0 all-to-all-done.got_ref
  22.4 0.0 copy-done.1
  22.4 0.0 copy-done
  22.4 1.3 %shard_map.97 = bf16[128,128]{1,0:T(8,128)(2,1)} custom-call(bf16[16,32,384]{2,1,0:T(8,128)(2,1)S(1)} %all-to-all-done.got_ref, bf16[10,128,512]{2,1,0:T(8,128)(2,1)S(1)} %bitcast.8, bf16[512,128]{1,0:T(8,128)(2,1)S(1)} %copy-done.1), custom_call_target="tpu_custom_call" | custom-call | flops 184549376 | bytes 2097152 | tf_op jit(solution)/shard_map/pallas_call | solution.py:201
  23.7 13.2 %all-to-all-start.1 = ((bf16[32,4,128]{2,1,0:T(4,128)(2,1)}), bf16[32,4,128]{2,1,0:T(4,128)(2,1)S(1)}, u32[]{:S(2)}, u32[]{:S(2)}) async-start(bf16[32,4,128]{2,1,0:T(4,128)(2,1)} %bitcast.5), calls=%async_computation.1 | async-start | bytes 65536 | tf_op jit(solution)/shard_map/all_to_all | solution.py:206
  36.9 0.0 collective-permute-done.2.x3
  36.9 0.0 collective-permute-done.1.x2
  36.9 0.0 collective-permute-done.x1
  37.0 0.0 copy-done.2
  37.0 0.0 copy-done.3
  37.0 4.5 %shard_map.95 = bf16[10,32,512]{2,1,0:T(8,128)(2,1)} custom-call(s32[1]{0:T(128)} %bitcast.lev_ref, bf16[10,32,512]{2,1,0:T(8,128)(2,1)S(1)} %copy-done.3, bf16[10,32,512]{2,1,0:T(8,128)(2,1)} %collective-permute-done.x1, bf16[10,32,512]{2,1,0:T(8,128)(2,1)} %collective-permute-done.1.x2, bf16[10,32,512]{2,1,0:T(8,128)(2,1)} %collective-permute-done.2.x3, ...), custom_call_target="tpu_custom_call" | custom-call | flops 1543503872 | bytes 5242880 | tf_op jit(solution)/shard_map/pallas_call | solution.py:211
  41.4 0.0 all-to-all-done.1
  41.5 1.0 %shard_map.98 = bf16[64,128]{1,0:T(8,128)(2,1)} custom-call(bf16[128,128]{1,0:T(8,128)(2,1)S(1)} %bitcast.9), custom_call_target="tpu_custom_call" | custom-call | flops 4194304 | bytes 65536 | tf_op jit(solution)/shard_map/pallas_call | solution.py:227
Async XLA Ops:
  0.6 21.7 %copy-start.1 = (bf16[512,128]{1,0:T(8,128)(2,1)S(1)}, bf16[512,128]{1,0:T(8,128)(2,1)}, u32[]{:S(2)}) copy-start(bf16[512,128]{1,0:T(8,128)(2,1)} %wout_ref.1) | copy-start | bytes 393220
  0.6 21.7 %copy-start = (bf16[1280,512]{1,0:T(8,128)(2,1)S(1)}, bf16[1280,512]{1,0:T(8,128)(2,1)}, u32[]{:S(2)}) copy-start(bf16[1280,512]{1,0:T(8,128)(2,1)} %sin.1) | copy-start | bytes 3932164
  2.9 34.0 %copy-start.2 = (bf16[1280,512]{1,0:T(8,128)(2,1)S(1)}, bf16[1280,512]{1,0:T(8,128)(2,1)}, u32[]{:S(2)}) copy-start(bf16[1280,512]{1,0:T(8,128)(2,1)} %gin.1) | copy-start | bytes 3932164
  3.0 34.0 %copy-start.3 = (bf16[10,32,512]{2,1,0:T(8,128)(2,1)S(1)}, bf16[10,32,512]{2,1,0:T(8,128)(2,1)}, u32[]{:S(2)}) copy-start(bf16[10,32,512]{2,1,0:T(8,128)(2,1)} %state_hbm.1) | copy-start | bytes 983044
  3.0 19.4 %all-to-all-start = ((bf16[16,32,384]{2,1,0:T(8,128)(2,1)}), bf16[16,32,384]{2,1,0:T(8,128)(2,1)S(1)}, u32[]{:S(2)}, u32[]{:S(2)}) async-start(bf16[16,32,384]{2,1,0:T(8,128)(2,1)} %bitcast.3), calls=%async_computation | async-start | bytes 786432 | tf_op jit(solution)/shard_map/all_to_all | solution.py:196
  13.4 23.6 %collective-permute-start.2 = (bf16[10,32,512]{2,1,0:T(8,128)(2,1)}, bf16[10,32,512]{2,1,0:T(8,128)(2,1)}, u32[]{:S(2)}, u32[]{:S(2)}) collective-permute-start(bf16[10,32,512]{2,1,0:T(8,128)(2,1)} %state_hbm.1), channel_id=1, source_target_pairs={{0,3},{1,2},{2,1},{3,0},{4,7},{5,6},{6,5},{7,4},{8,11},{9,10},{10,... | collective-permute-start | bytes 983048 | tf_op jit(solution)/shard_map/ppermute | solution.py:199
  17.9 19.1 %collective-permute-start.1 = (bf16[10,32,512]{2,1,0:T(8,128)(2,1)}, bf16[10,32,512]{2,1,0:T(8,128)(2,1)}, u32[]{:S(2)}, u32[]{:S(2)}) collective-permute-start(bf16[10,32,512]{2,1,0:T(8,128)(2,1)} %state_hbm.1), channel_id=1, source_target_pairs={{0,2},{1,3},{2,0},{3,1},{4,6},{5,7},{6,4},{7,5},{8,10},{9,11},{10,... | collective-permute-start | bytes 983048 | tf_op jit(solution)/shard_map/ppermute | solution.py:199
  20.3 16.6 %collective-permute-start = (bf16[10,32,512]{2,1,0:T(8,128)(2,1)}, bf16[10,32,512]{2,1,0:T(8,128)(2,1)}, u32[]{:S(2)}, u32[]{:S(2)}) collective-permute-start(bf16[10,32,512]{2,1,0:T(8,128)(2,1)} %state_hbm.1), channel_id=1, source_target_pairs={{0,1},{1,0},{2,3},{3,2},{4,5},{5,4},{6,7},{7,6},{8,9},{9,8},{10,11... | collective-permute-start | bytes 983048 | tf_op jit(solution)/shard_map/ppermute | solution.py:199
  23.7 17.8 %all-to-all-start.1 = ((bf16[32,4,128]{2,1,0:T(4,128)(2,1)}), bf16[32,4,128]{2,1,0:T(4,128)(2,1)S(1)}, u32[]{:S(2)}, u32[]{:S(2)}) async-start(bf16[32,4,128]{2,1,0:T(4,128)(2,1)} %bitcast.5), calls=%async_computation.1 | async-start | bytes 65536 | tf_op jit(solution)/shard_map/all_to_all | solution.py:206

commit v5 on v4

--- a/solution.py
+++ b/solution.py
@@ -95,16 +95,14 @@
     sources, levels = got_ref.shape
     row, col = iota((sources, sources), 0), iota((sources, sources), 1)
     picks = out_ref.shape[0]
-    got = got_ref[...].astype(F32)
-    lit = got < 0.5 * DARK
-    heat = jnp.where(lit, got, 0.0).astype(BF16)
-    lit_col = jnp.where(lit[:, :1], 1.0, 0.0)
+    got = got_ref[...]
+    lit_col = jnp.where(got[:, :1].astype(F32) < 0.5 * DARK, 1.0, 0.0)
     turn = sources - HEAD * GROUP
     place = [jnp.where(i < turn, i + HEAD * GROUP, i - turn) for i in (row, col)]
     below = onehot(place[1] < place[0])
     rank = matmul(below, jnp.broadcast_to(lit_col, (sources, picks)).astype(BF16))
     choose = jnp.where(rank == iota((sources, picks), 1).astype(F32), lit_col, 0.0).astype(BF16)
-    out_ref[...] = matmul(choose, heat, ((0,), (0,))).astype(BF16)
+    out_ref[...] = matmul(choose, got, ((0,), (0,))).astype(BF16)
 
 
 def tendency_kernel(

time: 43.1 us -> 43.1 us (level)
  no operation moved by 1% of the time
where the time goes in v5:
time: 43.1 us; the launch traced here: 42.4 us
  starting transfers between devices  32.6 us (76%)
  Pallas kernels  9.04 us (21%)
  between operations  0.79 us (2%)
    all_to_all x1, starting transfers between devices, local(): lax.all_to_all(heat.reshape(slots, GROUP, levels), 'col', 0, 0, tiled=Tru...  13.2 us
    all_to_all x1, starting transfers between devices, local(): lax.all_to_all(packed, ('col', 'lev'), 0, 0, tiled=True, axis_index_group...  10.4 us
    ppermute x3, starting transfers between devices, local(): lax.ppermute(state, 'lev', ring[step])  8.98 us
    pallas_call x1, Pallas kernels, local(): call(tendency_kernel, ((fields, part, cols), BF16), (2 * cols * (fields *...  4.46 us
    pallas_call x1, Pallas kernels, local(): call(pack_kernel, ((cols, WIDE), BF16), (2 * cols * cols * WIDE, 1 << 20)...  2.29 us
    pallas_call x1, Pallas kernels, local(): call(heat_kernel, ((slots * GROUP, levels), BF16), (2 * blocks * (fields...  1.3 us
    pallas_call x1, Pallas kernels, local(): call(pick_kernel, ((blocks // 2, levels), BF16), (1 << 22, 1 << 16), 'v')  0.99 us
  transfers between devices with their start and end apart: 5, of which 0 were waited for; matrix products, arithmetic and copies ran while one was open for 0% of the time, Pallas kernels for 14%

profile of v5, /device:TPU:1, one launch (start us, length us, event | category | flops | bytes accessed | tf_op | source)
XLA Modules:
  0.0 42.4 jit_solution(18019311850363692939)
XLA Ops:
  0.6 0.0 copy-start.1
  0.6 0.0 copy-start
  0.7 2.3 %shard_map.96 = bf16[512,384]{1,0:T(8,128)(2,1)} custom-call(bf16[10,32,512]{2,1,0:T(8,128)(2,1)} %state_hbm.1, s32[1,128]{1,0:T(1,128)} %bitcast.11, s32[1,128]{1,0:T(1,128)} %bitcast.12), custom_call_target="tpu_custom_call" | custom-call | flops 201326592 | bytes 1048576 | tf_op jit(solution)/shard_map/pallas_call | solution.py:182
  2.9 0.0 copy-start.2
  3.0 0.0 copy-start.3
  3.0 10.4 %all-to-all-start = ((bf16[16,32,384]{2,1,0:T(8,128)(2,1)}), bf16[16,32,384]{2,1,0:T(8,128)(2,1)S(1)}, u32[]{:S(2)}, u32[]{:S(2)}) async-start(bf16[16,32,384]{2,1,0:T(8,128)(2,1)} %bitcast.3), calls=%async_computation | async-start | bytes 786432 | tf_op jit(solution)/shard_map/all_to_all | solution.py:194
  13.4 4.5 %collective-permute-start.2 = (bf16[10,32,512]{2,1,0:T(8,128)(2,1)}, bf16[10,32,512]{2,1,0:T(8,128)(2,1)}, u32[]{:S(2)}, u32[]{:S(2)}) collective-permute-start(bf16[10,32,512]{2,1,0:T(8,128)(2,1)} %state_hbm.1), channel_id=1, source_target_pairs={{0,3},{1,2},{2,1},{3,0},{4,7},{5,6},{6,5},{7,4},{8,11},{9,10},{10,... | collective-permute-start | bytes 983048 | tf_op jit(solution)/shard_map/ppermute | solution.py:197
  17.9 2.5 %collective-permute-start.1 = (bf16[10,32,512]{2,1,0:T(8,128)(2,1)}, bf16[10,32,512]{2,1,0:T(8,128)(2,1)}, u32[]{:S(2)}, u32[]{:S(2)}) collective-permute-start(bf16[10,32,512]{2,1,0:T(8,128)(2,1)} %state_hbm.1), channel_id=1, source_target_pairs={{0,2},{1,3},{2,0},{3,1},{4,6},{5,7},{6,4},{7,5},{8,10},{9,11},{10,... | collective-permute-start | bytes 983048 | tf_op jit(solution)/shard_map/ppermute | solution.py:197
  20.3 2.0 %collective-permute-start = (bf16[10,32,512]{2,1,0:T(8,128)(2,1)}, bf16[10,32,512]{2,1,0:T(8,128)(2,1)}, u32[]{:S(2)}, u32[]{:S(2)}) collective-permute-start(bf16[10,32,512]{2,1,0:T(8,128)(2,1)} %state_hbm.1), channel_id=1, source_target_pairs={{0,1},{1,0},{2,3},{3,2},{4,5},{5,4},{6,7},{7,6},{8,9},{9,8},{10,11... | collective-permute-start | bytes 983048 | tf_op jit(solution)/shard_map/ppermute | solution.py:197
  22.4 0.0 all-to-all-done.got_ref
  22.4 0.0 copy-done.1
  22.4 0.0 copy-done
  22.4 1.3 %shard_map.97 = bf16[128,128]{1,0:T(8,128)(2,1)} custom-call(bf16[16,32,384]{2,1,0:T(8,128)(2,1)S(1)} %all-to-all-done.got_ref, bf16[10,128,512]{2,1,0:T(8,128)(2,1)S(1)} %bitcast.8, bf16[512,128]{1,0:T(8,128)(2,1)S(1)} %copy-done.1), custom_call_target="tpu_custom_call" | custom-call | flops 184549376 | bytes 2097152 | tf_op jit(solution)/shard_map/pallas_call | solution.py:199
  23.7 13.2 %all-to-all-start.1 = ((bf16[32,4,128]{2,1,0:T(4,128)(2,1)}), bf16[32,4,128]{2,1,0:T(4,128)(2,1)S(1)}, u32[]{:S(2)}, u32[]{:S(2)}) async-start(bf16[32,4,128]{2,1,0:T(4,128)(2,1)} %bitcast.5), calls=%async_computation.1 | async-start | bytes 65536 | tf_op jit(solution)/shard_map/all_to_all | solution.py:204
  36.9 0.0 collective-permute-done.2.x3
  36.9 0.0 collective-permute-done.1.x2
  36.9 0.0 collective-permute-done.x1
  37.0 0.0 copy-done.2
  37.0 0.0 copy-done.3
  37.0 4.5 %shard_map.95 = bf16[10,32,512]{2,1,0:T(8,128)(2,1)} custom-call(s32[1]{0:T(128)} %bitcast.lev_ref, bf16[10,32,512]{2,1,0:T(8,128)(2,1)S(1)} %copy-done.3, bf16[10,32,512]{2,1,0:T(8,128)(2,1)} %collective-permute-done.x1, bf16[10,32,512]{2,1,0:T(8,128)(2,1)} %collective-permute-done.1.x2, bf16[10,32,512]{2,1,0:T(8,128)(2,1)} %collective-permute-done.2.x3, ...), custom_call_target="tpu_custom_call" | custom-call | flops 1543503872 | bytes 5242880 | tf_op jit(solution)/shard_map/pallas_call | solution.py:209
  41.4 0.0 all-to-all-done.1
  41.5 1.0 %shard_map.98 = bf16[64,128]{1,0:T(8,128)(2,1)} custom-call(bf16[128,128]{1,0:T(8,128)(2,1)S(1)} %bitcast.9), custom_call_target="tpu_custom_call" | custom-call | flops 4194304 | bytes 65536 | tf_op jit(solution)/shard_map/pallas_call | solution.py:225
Async XLA Ops:
  0.6 21.7 %copy-start.1 = (bf16[512,128]{1,0:T(8,128)(2,1)S(1)}, bf16[512,128]{1,0:T(8,128)(2,1)}, u32[]{:S(2)}) copy-start(bf16[512,128]{1,0:T(8,128)(2,1)} %wout_ref.1) | copy-start | bytes 393220
  0.6 21.7 %copy-start = (bf16[1280,512]{1,0:T(8,128)(2,1)S(1)}, bf16[1280,512]{1,0:T(8,128)(2,1)}, u32[]{:S(2)}) copy-start(bf16[1280,512]{1,0:T(8,128)(2,1)} %sin.1) | copy-start | bytes 3932164
  2.9 34.0 %copy-start.2 = (bf16[1280,512]{1,0:T(8,128)(2,1)S(1)}, bf16[1280,512]{1,0:T(8,128)(2,1)}, u32[]{:S(2)}) copy-start(bf16[1280,512]{1,0:T(8,128)(2,1)} %gin.1) | copy-start | bytes 3932164
  3.0 34.0 %copy-start.3 = (bf16[10,32,512]{2,1,0:T(8,128)(2,1)S(1)}, bf16[10,32,512]{2,1,0:T(8,128)(2,1)}, u32[]{:S(2)}) copy-start(bf16[10,32,512]{2,1,0:T(8,128)(2,1)} %state_hbm.1) | copy-start | bytes 983044
  3.0 19.4 %all-to-all-start = ((bf16[16,32,384]{2,1,0:T(8,128)(2,1)}), bf16[16,32,384]{2,1,0:T(8,128)(2,1)S(1)}, u32[]{:S(2)}, u32[]{:S(2)}) async-start(bf16[16,32,384]{2,1,0:T(8,128)(2,1)} %bitcast.3), calls=%async_computation | async-start | bytes 786432 | tf_op jit(solution)/shard_map/all_to_all | solution.py:194
  13.4 23.6 %collective-permute-start.2 = (bf16[10,32,512]{2,1,0:T(8,128)(2,1)}, bf16[10,32,512]{2,1,0:T(8,128)(2,1)}, u32[]{:S(2)}, u32[]{:S(2)}) collective-permute-start(bf16[10,32,512]{2,1,0:T(8,128)(2,1)} %state_hbm.1), channel_id=1, source_target_pairs={{0,3},{1,2},{2,1},{3,0},{4,7},{5,6},{6,5},{7,4},{8,11},{9,10},{10,... | collective-permute-start | bytes 983048 | tf_op jit(solution)/shard_map/ppermute | solution.py:197
  17.9 19.1 %collective-permute-start.1 = (bf16[10,32,512]{2,1,0:T(8,128)(2,1)}, bf16[10,32,512]{2,1,0:T(8,128)(2,1)}, u32[]{:S(2)}, u32[]{:S(2)}) collective-permute-start(bf16[10,32,512]{2,1,0:T(8,128)(2,1)} %state_hbm.1), channel_id=1, source_target_pairs={{0,2},{1,3},{2,0},{3,1},{4,6},{5,7},{6,4},{7,5},{8,10},{9,11},{10,... | collective-permute-start | bytes 983048 | tf_op jit(solution)/shard_map/ppermute | solution.py:197
  20.3 16.6 %collective-permute-start = (bf16[10,32,512]{2,1,0:T(8,128)(2,1)}, bf16[10,32,512]{2,1,0:T(8,128)(2,1)}, u32[]{:S(2)}, u32[]{:S(2)}) collective-permute-start(bf16[10,32,512]{2,1,0:T(8,128)(2,1)} %state_hbm.1), channel_id=1, source_target_pairs={{0,1},{1,0},{2,3},{3,2},{4,5},{5,4},{6,7},{7,6},{8,9},{9,8},{10,11... | collective-permute-start | bytes 983048 | tf_op jit(solution)/shard_map/ppermute | solution.py:197
  23.7 17.8 %all-to-all-start.1 = ((bf16[32,4,128]{2,1,0:T(4,128)(2,1)}), bf16[32,4,128]{2,1,0:T(4,128)(2,1)S(1)}, u32[]{:S(2)}, u32[]{:S(2)}) async-start(bf16[32,4,128]{2,1,0:T(4,128)(2,1)} %bitcast.5), calls=%async_computation.1 | async-start | bytes 65536 | tf_op jit(solution)/shard_map/all_to_all | solution.py:204

commit v6 on v4

--- a/solution.py
+++ b/solution.py
@@ -129,8 +129,11 @@
     for copy in copies:
         copy.start()
     own = pl.multiple_of(lev * part, part)
-    for copy in copies[: levs + 1]:
+    for copy in copies[:levs]:
         copy.wait()
+    flat = whole[...].reshape(fields * levels, cols)
+    hidden = jnp.tanh(matmul(flat, gin[...], ((0,), (0,)))).astype(BF16)
+    copies[levs].wait()
     for field in range(fields):
         term = matmul(coupling[field, pl.ds(own, part), :], whole[field])
         if field < 3:
@@ -139,8 +142,6 @@
             out[field] = term.astype(BF16)
     first = pltpu.make_async_copy(out.at[3:], out_hbm.at[3:], sems.at[len(copies)])
     first.start()
-    flat = whole[...].reshape(fields * levels, cols)
-    hidden = jnp.tanh(matmul(flat, gin[...], ((0,), (0,)))).astype(BF16)
     copies[levs + 1].wait()
     drag[: 2 * levels] = matmul(gout[...], hidden, ((0,), (1,)))
     hidden = jnp.tanh(matmul(flat, sin[...], ((0,), (0,)))).astype(BF16)

time: 43.1 us -> 43.1 us (level)
  no operation moved by 1% of the time
where the time goes in v6:
time: 43.1 us; the launch traced here: 42.5 us
  starting transfers between devices  32.6 us (76%)
  Pallas kernels  9.09 us (21%)
  between operations  0.79 us (2%)
    all_to_all x1, starting transfers between devices, local(): lax.all_to_all(heat.reshape(slots, GROUP, levels), 'col', 0, 0, tiled=Tru...  13.2 us
    all_to_all x1, starting transfers between devices, local(): lax.all_to_all(packed, ('col', 'lev'), 0, 0, tiled=True, axis_index_group...  10.4 us
    ppermute x3, starting transfers between devices, local(): lax.ppermute(state, 'lev', ring[step])  8.98 us
    pallas_call x1, Pallas kernels, local(): call(tendency_kernel, ((fields, part, cols), BF16), (2 * cols * (fields *...  4.51 us
    pallas_call x1, Pallas kernels, local(): call(pack_kernel, ((cols, WIDE), BF16), (2 * cols * cols * WIDE, 1 << 20)...  2.29 us
    pallas_call x1, Pallas kernels, local(): call(heat_kernel, ((slots * GROUP, levels), BF16), (2 * blocks * (fields...  1.3 us
    pallas_call x1, Pallas kernels, local(): call(pick_kernel, ((blocks // 2, levels), BF16), (1 << 22, 1 << 16), 'v')  0.99 us
  transfers between devices with their start and end apart: 5, of which 0 were waited for; matrix products, arithmetic and copies ran while one was open for 0% of the time, Pallas kernels for 14%

profile of v6, /device:TPU:1, one launch (start us, length us, event | category | flops | bytes accessed | tf_op | source)
XLA Modules:
  0.0 42.5 jit_solution(6831109155622413744)
XLA Ops:
  0.6 0.0 copy-start.1
  0.6 0.0 copy-start
  0.7 2.3 %shard_map.96 = bf16[512,384]{1,0:T(8,128)(2,1)} custom-call(bf16[10,32,512]{2,1,0:T(8,128)(2,1)} %state_hbm.1, s32[1,128]{1,0:T(1,128)} %bitcast.11, s32[1,128]{1,0:T(1,128)} %bitcast.12), custom_call_target="tpu_custom_call" | custom-call | flops 201326592 | bytes 1048576 | tf_op jit(solution)/shard_map/pallas_call | solution.py:185
  2.9 0.0 copy-start.2
  3.0 0.0 copy-start.3
  3.0 10.4 %all-to-all-start = ((bf16[16,32,384]{2,1,0:T(8,128)(2,1)}), bf16[16,32,384]{2,1,0:T(8,128)(2,1)S(1)}, u32[]{:S(2)}, u32[]{:S(2)}) async-start(bf16[16,32,384]{2,1,0:T(8,128)(2,1)} %bitcast.3), calls=%async_computation | async-start | bytes 786432 | tf_op jit(solution)/shard_map/all_to_all | solution.py:197
  13.4 4.5 %collective-permute-start.2 = (bf16[10,32,512]{2,1,0:T(8,128)(2,1)}, bf16[10,32,512]{2,1,0:T(8,128)(2,1)}, u32[]{:S(2)}, u32[]{:S(2)}) collective-permute-start(bf16[10,32,512]{2,1,0:T(8,128)(2,1)} %state_hbm.1), channel_id=1, source_target_pairs={{0,3},{1,2},{2,1},{3,0},{4,7},{5,6},{6,5},{7,4},{8,11},{9,10},{10,... | collective-permute-start | bytes 983048 | tf_op jit(solution)/shard_map/ppermute | solution.py:200
  17.9 2.5 %collective-permute-start.1 = (bf16[10,32,512]{2,1,0:T(8,128)(2,1)}, bf16[10,32,512]{2,1,0:T(8,128)(2,1)}, u32[]{:S(2)}, u32[]{:S(2)}) collective-permute-start(bf16[10,32,512]{2,1,0:T(8,128)(2,1)} %state_hbm.1), channel_id=1, source_target_pairs={{0,2},{1,3},{2,0},{3,1},{4,6},{5,7},{6,4},{7,5},{8,10},{9,11},{10,... | collective-permute-start | bytes 983048 | tf_op jit(solution)/shard_map/ppermute | solution.py:200
  20.3 2.0 %collective-permute-start = (bf16[10,32,512]{2,1,0:T(8,128)(2,1)}, bf16[10,32,512]{2,1,0:T(8,128)(2,1)}, u32[]{:S(2)}, u32[]{:S(2)}) collective-permute-start(bf16[10,32,512]{2,1,0:T(8,128)(2,1)} %state_hbm.1), channel_id=1, source_target_pairs={{0,1},{1,0},{2,3},{3,2},{4,5},{5,4},{6,7},{7,6},{8,9},{9,8},{10,11... | collective-permute-start | bytes 983048 | tf_op jit(solution)/shard_map/ppermute | solution.py:200
  22.4 0.0 all-to-all-done.got_ref
  22.4 0.0 copy-done.1
  22.4 0.0 copy-done
  22.4 1.3 %shard_map.97 = bf16[128,128]{1,0:T(8,128)(2,1)} custom-call(bf16[16,32,384]{2,1,0:T(8,128)(2,1)S(1)} %all-to-all-done.got_ref, bf16[10,128,512]{2,1,0:T(8,128)(2,1)S(1)} %bitcast.8, bf16[512,128]{1,0:T(8,128)(2,1)S(1)} %copy-done.1), custom_call_target="tpu_custom_call" | custom-call | flops 184549376 | bytes 2097152 | tf_op jit(solution)/shard_map/pallas_call | solution.py:202
  23.7 13.2 %all-to-all-start.1 = ((bf16[32,4,128]{2,1,0:T(4,128)(2,1)}), bf16[32,4,128]{2,1,0:T(4,128)(2,1)S(1)}, u32[]{:S(2)}, u32[]{:S(2)}) async-start(bf16[32,4,128]{2,1,0:T(4,128)(2,1)} %bitcast.5), calls=%async_computation.1 | async-start | bytes 65536 | tf_op jit(solution)/shard_map/all_to_all | solution.py:207
  36.9 0.0 collective-permute-done.2.x3
  36.9 0.0 collective-permute-done.1.x2
  36.9 0.0 collective-permute-done.x1
  37.0 0.0 copy-done.2
  37.0 0.0 copy-done.3
  37.0 4.5 %shard_map.95 = bf16[10,32,512]{2,1,0:T(8,128)(2,1)} custom-call(s32[1]{0:T(128)} %bitcast.lev_ref, bf16[10,32,512]{2,1,0:T(8,128)(2,1)S(1)} %copy-done.3, bf16[10,32,512]{2,1,0:T(8,128)(2,1)} %collective-permute-done.x1, bf16[10,32,512]{2,1,0:T(8,128)(2,1)} %collective-permute-done.1.x2, bf16[10,32,512]{2,1,0:T(8,128)(2,1)} %collective-permute-done.2.x3, ...), custom_call_target="tpu_custom_call" | custom-call | flops 1543503872 | bytes 5242880 | tf_op jit(solution)/shard_map/pallas_call | solution.py:212
  41.5 0.0 all-to-all-done.1
  41.5 1.0 %shard_map.98 = bf16[64,128]{1,0:T(8,128)(2,1)} custom-call(bf16[128,128]{1,0:T(8,128)(2,1)S(1)} %bitcast.9), custom_call_target="tpu_custom_call" | custom-call | flops 4194304 | bytes 65536 | tf_op jit(solution)/shard_map/pallas_call | solution.py:228
Async XLA Ops:
  0.6 21.7 %copy-start.1 = (bf16[512,128]{1,0:T(8,128)(2,1)S(1)}, bf16[512,128]{1,0:T(8,128)(2,1)}, u32[]{:S(2)}) copy-start(bf16[512,128]{1,0:T(8,128)(2,1)} %wout_ref.1) | copy-start | bytes 393220
  0.6 21.7 %copy-start = (bf16[1280,512]{1,0:T(8,128)(2,1)S(1)}, bf16[1280,512]{1,0:T(8,128)(2,1)}, u32[]{:S(2)}) copy-start(bf16[1280,512]{1,0:T(8,128)(2,1)} %sin.1) | copy-start | bytes 3932164
  2.9 34.0 %copy-start.2 = (bf16[1280,512]{1,0:T(8,128)(2,1)S(1)}, bf16[1280,512]{1,0:T(8,128)(2,1)}, u32[]{:S(2)}) copy-start(bf16[1280,512]{1,0:T(8,128)(2,1)} %gin.1) | copy-start | bytes 3932164
  3.0 34.0 %copy-start.3 = (bf16[10,32,512]{2,1,0:T(8,128)(2,1)S(1)}, bf16[10,32,512]{2,1,0:T(8,128)(2,1)}, u32[]{:S(2)}) copy-start(bf16[10,32,512]{2,1,0:T(8,128)(2,1)} %state_hbm.1) | copy-start | bytes 983044
  3.0 19.4 %all-to-all-start = ((bf16[16,32,384]{2,1,0:T(8,128)(2,1)}), bf16[16,32,384]{2,1,0:T(8,128)(2,1)S(1)}, u32[]{:S(2)}, u32[]{:S(2)}) async-start(bf16[16,32,384]{2,1,0:T(8,128)(2,1)} %bitcast.3), calls=%async_computation | async-start | bytes 786432 | tf_op jit(solution)/shard_map/all_to_all | solution.py:197
  13.4 23.6 %collective-permute-start.2 = (bf16[10,32,512]{2,1,0:T(8,128)(2,1)}, bf16[10,32,512]{2,1,0:T(8,128)(2,1)}, u32[]{:S(2)}, u32[]{:S(2)}) collective-permute-start(bf16[10,32,512]{2,1,0:T(8,128)(2,1)} %state_hbm.1), channel_id=1, source_target_pairs={{0,3},{1,2},{2,1},{3,0},{4,7},{5,6},{6,5},{7,4},{8,11},{9,10},{10,... | collective-permute-start | bytes 983048 | tf_op jit(solution)/shard_map/ppermute | solution.py:200
  17.9 19.1 %collective-permute-start.1 = (bf16[10,32,512]{2,1,0:T(8,128)(2,1)}, bf16[10,32,512]{2,1,0:T(8,128)(2,1)}, u32[]{:S(2)}, u32[]{:S(2)}) collective-permute-start(bf16[10,32,512]{2,1,0:T(8,128)(2,1)} %state_hbm.1), channel_id=1, source_target_pairs={{0,2},{1,3},{2,0},{3,1},{4,6},{5,7},{6,4},{7,5},{8,10},{9,11},{10,... | collective-permute-start | bytes 983048 | tf_op jit(solution)/shard_map/ppermute | solution.py:200
  20.3 16.6 %collective-permute-start = (bf16[10,32,512]{2,1,0:T(8,128)(2,1)}, bf16[10,32,512]{2,1,0:T(8,128)(2,1)}, u32[]{:S(2)}, u32[]{:S(2)}) collective-permute-start(bf16[10,32,512]{2,1,0:T(8,128)(2,1)} %state_hbm.1), channel_id=1, source_target_pairs={{0,1},{1,0},{2,3},{3,2},{4,5},{5,4},{6,7},{7,6},{8,9},{9,8},{10,11... | collective-permute-start | bytes 983048 | tf_op jit(solution)/shard_map/ppermute | solution.py:200
  23.7 17.8 %all-to-all-start.1 = ((bf16[32,4,128]{2,1,0:T(4,128)(2,1)}), bf16[32,4,128]{2,1,0:T(4,128)(2,1)S(1)}, u32[]{:S(2)}, u32[]{:S(2)}) async-start(bf16[32,4,128]{2,1,0:T(4,128)(2,1)} %bitcast.5), calls=%async_computation.1 | async-start | bytes 65536 | tf_op jit(solution)/shard_map/all_to_all | solution.py:207

commit v7 on v5

--- a/solution.py
+++ b/solution.py
@@ -127,8 +127,11 @@
     for copy in copies:
         copy.start()
     own = pl.multiple_of(lev * part, part)
-    for copy in copies[: levs + 1]:
+    for copy in copies[:levs]:
         copy.wait()
+    flat = whole[...].reshape(fields * levels, cols)
+    hidden = jnp.tanh(matmul(flat, gin[...], ((0,), (0,)))).astype(BF16)
+    copies[levs].wait()
     for field in range(fields):
         term = matmul(coupling[field, pl.ds(own, part), :], whole[field])
         if field < 3:
@@ -137,8 +140,6 @@
             out[field] = term.astype(BF16)
     first = pltpu.make_async_copy(out.at[3:], out_hbm.at[3:], sems.at[len(copies)])
     first.start()
-    flat = whole[...].reshape(fields * levels, cols)
-    hidden = jnp.tanh(matmul(flat, gin[...], ((0,), (0,)))).astype(BF16)
     copies[levs + 1].wait()
     drag[: 2 * levels] = matmul(gout[...], hidden, ((0,), (1,)))
     hidden = jnp.tanh(matmul(flat, sin[...], ((0,), (0,)))).astype(BF16)

time: 43.1 us -> 43.1 us (level)
  no operation moved by 1% of the time
where the time goes in v7:
time: 43.1 us; the launch traced here: 42.5 us
  starting transfers between devices  32.6 us (76%)
  Pallas kernels  9.09 us (21%)
  between operations  0.79 us (2%)
    all_to_all x1, starting transfers between devices, local(): lax.all_to_all(heat.reshape(slots, GROUP, levels), 'col', 0, 0, tiled=Tru...  13.2 us
    all_to_all x1, starting transfers between devices, local(): lax.all_to_all(packed, ('col', 'lev'), 0, 0, tiled=True, axis_index_group...  10.4 us
    ppermute x3, starting transfers between devices, local(): lax.ppermute(state, 'lev', ring[step])  8.98 us
    pallas_call x1, Pallas kernels, local(): call(tendency_kernel, ((fields, part, cols), BF16), (2 * cols * (fields *...  4.51 us
    pallas_call x1, Pallas kernels, local(): call(pack_kernel, ((cols, WIDE), BF16), (2 * cols * cols * WIDE, 1 << 20)...  2.29 us
    pallas_call x1, Pallas kernels, local(): call(heat_kernel, ((slots * GROUP, levels), BF16), (2 * blocks * (fields...  1.3 us
    pallas_call x1, Pallas kernels, local(): call(pick_kernel, ((blocks // 2, levels), BF16), (1 << 22, 1 << 16), 'v')  0.99 us
  transfers between devices with their start and end apart: 5, of which 0 were waited for; matrix products, arithmetic and copies ran while one was open for 0% of the time, Pallas kernels for 14%

profile of v7, /device:TPU:1, one launch (start us, length us, event | category | flops | bytes accessed | tf_op | source)
XLA Modules:
  0.0 42.5 jit_solution(578253490286505647)
XLA Ops:
  0.6 0.0 copy-start.1
  0.6 0.0 copy-start
  0.7 2.3 %shard_map.96 = bf16[512,384]{1,0:T(8,128)(2,1)} custom-call(bf16[10,32,512]{2,1,0:T(8,128)(2,1)} %state_hbm.1, s32[1,128]{1,0:T(1,128)} %bitcast.11, s32[1,128]{1,0:T(1,128)} %bitcast.12), custom_call_target="tpu_custom_call" | custom-call | flops 201326592 | bytes 1048576 | tf_op jit(solution)/shard_map/pallas_call | solution.py:183
  2.9 0.0 copy-start.2
  3.0 0.0 copy-start.3
  3.0 10.4 %all-to-all-start = ((bf16[16,32,384]{2,1,0:T(8,128)(2,1)}), bf16[16,32,384]{2,1,0:T(8,128)(2,1)S(1)}, u32[]{:S(2)}, u32[]{:S(2)}) async-start(bf16[16,32,384]{2,1,0:T(8,128)(2,1)} %bitcast.3), calls=%async_computation | async-start | bytes 786432 | tf_op jit(solution)/shard_map/all_to_all | solution.py:195
  13.4 4.5 %collective-permute-start.2 = (bf16[10,32,512]{2,1,0:T(8,128)(2,1)}, bf16[10,32,512]{2,1,0:T(8,128)(2,1)}, u32[]{:S(2)}, u32[]{:S(2)}) collective-permute-start(bf16[10,32,512]{2,1,0:T(8,128)(2,1)} %state_hbm.1), channel_id=1, source_target_pairs={{0,3},{1,2},{2,1},{3,0},{4,7},{5,6},{6,5},{7,4},{8,11},{9,10},{10,... | collective-permute-start | bytes 983048 | tf_op jit(solution)/shard_map/ppermute | solution.py:198
  17.9 2.5 %collective-permute-start.1 = (bf16[10,32,512]{2,1,0:T(8,128)(2,1)}, bf16[10,32,512]{2,1,0:T(8,128)(2,1)}, u32[]{:S(2)}, u32[]{:S(2)}) collective-permute-start(bf16[10,32,512]{2,1,0:T(8,128)(2,1)} %state_hbm.1), channel_id=1, source_target_pairs={{0,2},{1,3},{2,0},{3,1},{4,6},{5,7},{6,4},{7,5},{8,10},{9,11},{10,... | collective-permute-start | bytes 983048 | tf_op jit(solution)/shard_map/ppermute | solution.py:198
  20.3 2.0 %collective-permute-start = (bf16[10,32,512]{2,1,0:T(8,128)(2,1)}, bf16[10,32,512]{2,1,0:T(8,128)(2,1)}, u32[]{:S(2)}, u32[]{:S(2)}) collective-permute-start(bf16[10,32,512]{2,1,0:T(8,128)(2,1)} %state_hbm.1), channel_id=1, source_target_pairs={{0,1},{1,0},{2,3},{3,2},{4,5},{5,4},{6,7},{7,6},{8,9},{9,8},{10,11... | collective-permute-start | bytes 983048 | tf_op jit(solution)/shard_map/ppermute | solution.py:198
  22.4 0.0 all-to-all-done.got_ref
  22.4 0.0 copy-done.1
  22.4 0.0 copy-done
  22.4 1.3 %shard_map.97 = bf16[128,128]{1,0:T(8,128)(2,1)} custom-call(bf16[16,32,384]{2,1,0:T(8,128)(2,1)S(1)} %all-to-all-done.got_ref, bf16[10,128,512]{2,1,0:T(8,128)(2,1)S(1)} %bitcast.8, bf16[512,128]{1,0:T(8,128)(2,1)S(1)} %copy-done.1), custom_call_target="tpu_custom_call" | custom-call | flops 184549376 | bytes 2097152 | tf_op jit(solution)/shard_map/pallas_call | solution.py:200
  23.7 13.2 %all-to-all-start.1 = ((bf16[32,4,128]{2,1,0:T(4,128)(2,1)}), bf16[32,4,128]{2,1,0:T(4,128)(2,1)S(1)}, u32[]{:S(2)}, u32[]{:S(2)}) async-start(bf16[32,4,128]{2,1,0:T(4,128)(2,1)} %bitcast.5), calls=%async_computation.1 | async-start | bytes 65536 | tf_op jit(solution)/shard_map/all_to_all | solution.py:205
  36.9 0.0 collective-permute-done.2.x3
  36.9 0.0 collective-permute-done.1.x2
  36.9 0.0 collective-permute-done.x1
  37.0 0.0 copy-done.2
  37.0 0.0 copy-done.3
  37.0 4.5 %shard_map.95 = bf16[10,32,512]{2,1,0:T(8,128)(2,1)} custom-call(s32[1]{0:T(128)} %bitcast.lev_ref, bf16[10,32,512]{2,1,0:T(8,128)(2,1)S(1)} %copy-done.3, bf16[10,32,512]{2,1,0:T(8,128)(2,1)} %collective-permute-done.x1, bf16[10,32,512]{2,1,0:T(8,128)(2,1)} %collective-permute-done.1.x2, bf16[10,32,512]{2,1,0:T(8,128)(2,1)} %collective-permute-done.2.x3, ...), custom_call_target="tpu_custom_call" | custom-call | flops 1543503872 | bytes 5242880 | tf_op jit(solution)/shard_map/pallas_call | solution.py:210
  41.5 0.0 all-to-all-done.1
  41.5 1.0 %shard_map.98 = bf16[64,128]{1,0:T(8,128)(2,1)} custom-call(bf16[128,128]{1,0:T(8,128)(2,1)S(1)} %bitcast.9), custom_call_target="tpu_custom_call" | custom-call | flops 4194304 | bytes 65536 | tf_op jit(solution)/shard_map/pallas_call | solution.py:226
Async XLA Ops:
  0.6 21.7 %copy-start.1 = (bf16[512,128]{1,0:T(8,128)(2,1)S(1)}, bf16[512,128]{1,0:T(8,128)(2,1)}, u32[]{:S(2)}) copy-start(bf16[512,128]{1,0:T(8,128)(2,1)} %wout_ref.1) | copy-start | bytes 393220
  0.6 21.7 %copy-start = (bf16[1280,512]{1,0:T(8,128)(2,1)S(1)}, bf16[1280,512]{1,0:T(8,128)(2,1)}, u32[]{:S(2)}) copy-start(bf16[1280,512]{1,0:T(8,128)(2,1)} %sin.1) | copy-start | bytes 3932164
  2.9 34.0 %copy-start.2 = (bf16[1280,512]{1,0:T(8,128)(2,1)S(1)}, bf16[1280,512]{1,0:T(8,128)(2,1)}, u32[]{:S(2)}) copy-start(bf16[1280,512]{1,0:T(8,128)(2,1)} %gin.1) | copy-start | bytes 3932164
  3.0 34.0 %copy-start.3 = (bf16[10,32,512]{2,1,0:T(8,128)(2,1)S(1)}, bf16[10,32,512]{2,1,0:T(8,128)(2,1)}, u32[]{:S(2)}) copy-start(bf16[10,32,512]{2,1,0:T(8,128)(2,1)} %state_hbm.1) | copy-start | bytes 983044
  3.0 19.4 %all-to-all-start = ((bf16[16,32,384]{2,1,0:T(8,128)(2,1)}), bf16[16,32,384]{2,1,0:T(8,128)(2,1)S(1)}, u32[]{:S(2)}, u32[]{:S(2)}) async-start(bf16[16,32,384]{2,1,0:T(8,128)(2,1)} %bitcast.3), calls=%async_computation | async-start | bytes 786432 | tf_op jit(solution)/shard_map/all_to_all | solution.py:195
  13.4 23.6 %collective-permute-start.2 = (bf16[10,32,512]{2,1,0:T(8,128)(2,1)}, bf16[10,32,512]{2,1,0:T(8,128)(2,1)}, u32[]{:S(2)}, u32[]{:S(2)}) collective-permute-start(bf16[10,32,512]{2,1,0:T(8,128)(2,1)} %state_hbm.1), channel_id=1, source_target_pairs={{0,3},{1,2},{2,1},{3,0},{4,7},{5,6},{6,5},{7,4},{8,11},{9,10},{10,... | collective-permute-start | bytes 983048 | tf_op jit(solution)/shard_map/ppermute | solution.py:198
  17.9 19.1 %collective-permute-start.1 = (bf16[10,32,512]{2,1,0:T(8,128)(2,1)}, bf16[10,32,512]{2,1,0:T(8,128)(2,1)}, u32[]{:S(2)}, u32[]{:S(2)}) collective-permute-start(bf16[10,32,512]{2,1,0:T(8,128)(2,1)} %state_hbm.1), channel_id=1, source_target_pairs={{0,2},{1,3},{2,0},{3,1},{4,6},{5,7},{6,4},{7,5},{8,10},{9,11},{10,... | collective-permute-start | bytes 983048 | tf_op jit(solution)/shard_map/ppermute | solution.py:198
  20.3 16.6 %collective-permute-start = (bf16[10,32,512]{2,1,0:T(8,128)(2,1)}, bf16[10,32,512]{2,1,0:T(8,128)(2,1)}, u32[]{:S(2)}, u32[]{:S(2)}) collective-permute-start(bf16[10,32,512]{2,1,0:T(8,128)(2,1)} %state_hbm.1), channel_id=1, source_target_pairs={{0,1},{1,0},{2,3},{3,2},{4,5},{5,4},{6,7},{7,6},{8,9},{9,8},{10,11... | collective-permute-start | bytes 983048 | tf_op jit(solution)/shard_map/ppermute | solution.py:198
  23.7 17.8 %all-to-all-start.1 = ((bf16[32,4,128]{2,1,0:T(4,128)(2,1)}), bf16[32,4,128]{2,1,0:T(4,128)(2,1)S(1)}, u32[]{:S(2)}, u32[]{:S(2)}) async-start(bf16[32,4,128]{2,1,0:T(4,128)(2,1)} %bitcast.5), calls=%async_computation.1 | async-start | bytes 65536 | tf_op jit(solution)/shard_map/all_to_all | solution.py:205
